TPU v7x, 128 devices: a whole 4x4x4 slice. The times are simulated.
128 devices in a mesh: seq: 16 (over y_hi, x, core), tp: 8 (over z, y_lo).
Axes of the slice: x: 4, y: 4 (y_hi: 2, y_lo: 2; y = y_hi * 2 + y_lo), z: 4, core: 2. Of those that a mesh axis runs over, the one named last changes fastest.
Arguments:
- teacher_queries: bfloat16 [2048, 8192], P('seq', 'tp'), may hold values from -110 to 110
- teacher_kv: bfloat16 [2, 12288, 1024], P(None, 'seq', 'tp'), may hold values from -4 to 4
- student_queries: bfloat16 [2048, 4096], P('seq', 'tp'), may hold values from -110 to 110
- student_kv: bfloat16 [2, 12288, 1024], P(None, 'seq', 'tp'), may hold values from -4 to 4
- doc_start: int32 [1], replicated, may hold values from 0 to 5119
- teacher_resid: bfloat16 [2048, 8192], P('tp', 'seq'), may hold values from -0.75 to 0.75
- teacher_out_proj: bfloat16 [8192, 8192], P('tp', 'seq'), may hold values from -0.0625 to 0.0625
- teacher_gain: float32 [8192], P('seq'), may hold values from 0.1 to 1.9
- student_resid: bfloat16 [2048, 4096], P('tp', 'seq'), may hold values from -0.75 to 0.75
- student_out_proj: bfloat16 [4096, 4096], P('tp', 'seq'), may hold values from -0.09375 to 0.09375
- student_gain: float32 [4096], P('seq'), may hold values from 0.1 to 1.9
- match_proj: bfloat16 [4096, 8192], P(None, 'seq'), may hold values from -0.09375 to 0.09375
Outputs:
- match_grad: float32 [4096, 8192], P('tp', 'seq')
All inputs are finite; a program needn't handle non-finite values.
Results may differ from a plain program's by a relative error of at most 0.0055.
Values may be sent and summed in bfloat16 or wider, within the bound.
A program may use at most 192 MiB of HBM per device.

v0:
```python
import math

import jax
import jax.numpy as jnp
from jax import lax
from jax.sharding import PartitionSpec as P

D_T = 8192
D_S = 4096
HEAD = 128


def fold_piece(queries, query_index, first_key, carry, piece):
    count = piece.shape[1]
    kv_local = queries.shape[1]
    keys_piece = piece[0].reshape(count, kv_local, HEAD)
    values_piece = piece[1].reshape(count, kv_local, HEAD)
    scores = jnp.einsum(
        "tkgd,nkd->tkgn", queries, keys_piece, preferred_element_type=jnp.float32
    ) * (1.0 / math.sqrt(HEAD))
    key_index = jnp.arange(count, dtype=jnp.int32)
    visible = (key_index[None, :] <= query_index[:, None]) & (key_index[None, :] >= first_key)
    visible = visible[:, None, None, :]
    scores = jnp.where(visible, scores, -1e30)
    old_max, old_total, old_out = carry
    new_max = jnp.maximum(old_max, jnp.max(scores, axis=-1))
    weights = jnp.where(visible, jnp.exp(scores - new_max[..., None]), 0.0)
    total = jnp.sum(weights, axis=-1)
    values_sum = jnp.einsum(
        "tkgn,nkd->tkgd",
        weights.astype(jnp.bfloat16),
        values_piece,
        preferred_element_type=jnp.float32,
    )
    return (new_max, total, values_sum)


def start_carry(queries):
    shape = queries.shape[:3]
    return (
        jnp.full(shape, -1e30, jnp.float32),
        jnp.zeros(shape, jnp.float32),
        jnp.zeros(queries.shape, jnp.float32),
    )


def finish(carry, rows):
    context = carry[2] / carry[1][..., None]
    return context.astype(jnp.bfloat16).reshape(rows, -1)


def per_device(
    teacher_queries,
    teacher_kv,
    student_queries,
    student_kv,
    doc_start,
    teacher_resid,
    teacher_out_proj,
    teacher_gain,
    student_resid,
    student_out_proj,
    student_gain,
    match_proj,
):
    rows = teacher_queries.shape[0]
    seq_count = lax.axis_size("seq")
    slab_length = rows * seq_count
    cache_length = teacher_kv.shape[1] * seq_count - slab_length
    query_index = cache_length + lax.axis_index("seq") * rows + jnp.arange(rows, dtype=jnp.int32)
    first_key = doc_start[0]
    kv_local = teacher_kv.shape[2] // HEAD
    teacher_q = teacher_queries.reshape(rows, kv_local, -1, HEAD)
    student_q = student_queries.reshape(rows, kv_local, -1, HEAD)
    teacher_carry = fold_piece(
        teacher_q,
        query_index,
        first_key,
        start_carry(teacher_q),
        lax.all_gather(teacher_kv, "seq", axis=1, tiled=True),
    )
    student_carry = fold_piece(
        student_q,
        query_index,
        first_key,
        start_carry(student_q),
        lax.all_gather(student_kv, "seq", axis=1, tiled=True),
    )
    teacher_context = finish(teacher_carry, rows)
    student_context = finish(student_carry, rows)
    teacher_rows, student_rows = (
        lax.all_gather(teacher_context, "seq", axis=0, tiled=True),
        lax.all_gather(student_context, "seq", axis=0, tiled=True),
    )
    teacher_width = teacher_resid.shape[1]
    partial_sums = jnp.concatenate(
        [
            jnp.dot(teacher_rows, teacher_out_proj, preferred_element_type=jnp.float32),
            jnp.dot(student_rows, student_out_proj, preferred_element_type=jnp.float32),
        ],
        axis=1,
    )
    summed = lax.psum_scatter(partial_sums, "tp", scatter_dimension=0, tiled=True)
    teacher_hidden = teacher_resid.astype(jnp.float32) + summed[:, :teacher_width]
    student_hidden = student_resid.astype(jnp.float32) + summed[:, teacher_width:]
    teacher_squares, student_squares = lax.psum(
        (
            jnp.sum(teacher_hidden * teacher_hidden, axis=1),
            jnp.sum(student_hidden * student_hidden, axis=1),
        ),
        "seq",
    )
    teacher_scale = jnp.sqrt(teacher_squares / D_T + 1e-05)
    student_scale = jnp.sqrt(student_squares / D_S + 1e-05)
    target = teacher_hidden / teacher_scale[:, None] * teacher_gain
    normed = (student_hidden / student_scale[:, None] * student_gain).astype(jnp.bfloat16)
    full_normed = lax.all_gather(normed, "seq", axis=1, tiled=True)
    diff = jnp.dot(full_normed, match_proj, preferred_element_type=jnp.float32) - target
    delta = diff / math.sqrt(slab_length)
    wide_normed = full_normed.astype(jnp.float32)
    return lax.psum_scatter(
        lax.dot_general(
            wide_normed,
            delta,
            (((0,), (0,)), ((), ())),
            precision=lax.Precision.HIGHEST,
            preferred_element_type=jnp.float32,
        ),
        "tp",
        scatter_dimension=0,
        tiled=True,
    )


def solution(mesh):
    in_specs = (
        P("seq", "tp"),
        P(None, "seq", "tp"),
        P("seq", "tp"),
        P(None, "seq", "tp"),
        P(),
        P("tp", "seq"),
        P("tp", "seq"),
        P("seq"),
        P("tp", "seq"),
        P("tp", "seq"),
        P("seq"),
        P(None, "seq"),
    )
    out_specs = P("tp", "seq")
    return jax.shard_map(
        per_device, mesh=mesh, in_specs=in_specs, out_specs=out_specs, check_vma=False
    )
```

profile of v0, /device:TPU:0, one launch (start us, length us, event | category | flops | bytes accessed | tf_op | source)
XLA Modules:
  0.0 696.0 jit_solution(11219260860999022749)
XLA Ops:
  6.5 0.7 all-gather.6.cloned.1.call-update
  7.3 0.7 all-gather.10.cloned.1.call-update
  8.7 6.4 fusion.14
  15.1 61.4 %all-gather.6.cloned.1.call-done = bf16[2,12288,128]{2,1,0:T(8,128)(2,1)} async-done(((bf16[2,768,128]{2,1,0:T(8,128)(2,1)}), bf16[2,12288,128]{2,1,0:T(8,128)(2,1)}) %all-gather.6.cloned.1.call-update) | async-done | bytes 6291472 | tf_op jit(solution)/shard_map/all_gather | solution.py:80
  76.5 21.5 %fusion = (f32[128,8]{0,1:T(8,128)S(1)}, f32[12288,128,8]{1,0,2:T(8,128)}) fusion(pred[128,12288]{0,1:T(8,128)(4,1)S(1)} %fusion.14, bf16[2,12288,128]{2,1,0:T(8,128)(2,1)} %all-gather.6.cloned.1.call-done, bf16[128,1024]{1,0:T(8,128)(2,1)} %param.12), kind=kOutput, calls=%fused_computation.2 | convolution fusion | flops 3258973184 | bytes 55316480 | tf_op jit(solution)/shard_map/tkgd,nkd->tkgn/dot_general | solution.py:18
  98.0 43.6 %all-gather.10.cloned.1.call-done = bf16[2,12288,128]{2,1,0:T(8,128)(2,1)} async-done(((bf16[2,768,128]{2,1,0:T(8,128)(2,1)}), bf16[2,12288,128]{2,1,0:T(8,128)(2,1)}) %all-gather.10.cloned.1.call-update) | async-done | bytes 6291472 | tf_op jit(solution)/shard_map/all_gather | solution.py:87
  141.6 12.7 %fusion.7 = (f32[128,4]{0,1:T(4,128)S(1)}, f32[12288,128,4]{1,0,2:T(8,128)}) fusion(pred[128,12288]{0,1:T(8,128)(4,1)S(1)} %fusion.14, bf16[2,12288,128]{2,1,0:T(8,128)(2,1)} %all-gather.10.cloned.1.call-done, bf16[128,512]{1,0:T(8,128)(2,1)S(1)} %copy-done.6), kind=kOutput, calls=%fused_computation.10 | convolution fusion | flops 1629486592 | bytes 30017536 | tf_op jit(solution)/shard_map/tkgd,nkd->tkgn/dot_general | solution.py:18
  154.3 11.4 %fusion.8 = f32[128,4]{0,1:T(4,128)S(1)} fusion(f32[12288,128,4]{1,0,2:T(8,128)} %get-tuple-element.8, f32[128,4]{0,1:T(4,128)S(1)} %broadcast_maximum_fusion.1, pred[128,12288]{0,1:T(8,128)(4,1)S(1)} %fusion.14), kind=kLoop, calls=%fused_computation.11 | loop fusion | flops 31456768 | bytes 26742784 | tf_op jit(solution)/shard_map/reduce_sum | solution.py:28
  165.7 13.0 %fusion.33 = bf16[1,128,128,4]{2,1,3,0:T(8,128)(2,1)} fusion(bf16[2,12288,128]{2,1,0:T(8,128)(2,1)} %all-gather.10.cloned.1.call-done, f32[12288,128,4]{1,0,2:T(8,128)} %get-tuple-element.8, f32[128,4]{0,1:T(4,128)S(1)} %broadcast_maximum_fusion.1, pred[128,12288]{0,1:T(8,128)(4,1)S(1)} %fusion.14, f32[128,4]{0,1:T(4,128)S(1)} %fusion.8), kind=kOutput, calls=%fused_computation.32 | convolution fusion | flops 1642201088 | bytes 30019584 | tf_op jit(solution)/shard_map/tkgn,nkd->tkgd/dot_general | solution.py:29
  178.8 0.2 all-gather.8.cloned.1.call-start
  179.0 21.5 %fusion.1 = f32[128,8]{0,1:T(8,128)S(1)} fusion(f32[12288,128,8]{1,0,2:T(8,128)} %get-tuple-element.10, f32[128,8]{0,1:T(8,128)S(1)} %broadcast_maximum_fusion, pred[128,12288]{0,1:T(8,128)(4,1)S(1)} %fusion.14), kind=kLoop, calls=%fused_computation.3 | loop fusion | flops 62913536 | bytes 51912704 | tf_op jit(solution)/shard_map/reduce_sum | solution.py:28
  200.5 21.4 %fusion.27 = bf16[1,128,128,8]{2,1,3,0:T(8,128)(2,1)} fusion(bf16[2,12288,128]{2,1,0:T(8,128)(2,1)} %all-gather.6.cloned.1.call-done, f32[12288,128,8]{1,0,2:T(8,128)} %get-tuple-element.10, f32[128,8]{0,1:T(8,128)S(1)} %broadcast_maximum_fusion, pred[128,12288]{0,1:T(8,128)(4,1)S(1)} %fusion.14, f32[128,8]{0,1:T(8,128)S(1)} %fusion.1), kind=kOutput, calls=%fused_computation.30 | convolution fusion | flops 3284402176 | bytes 55320576 | tf_op jit(solution)/shard_map/tkgn,nkd->tkgd/dot_general | solution.py:29
  221.9 0.0 reduce-scatter.3.cloned.1.call-start
  222.0 4.9 all-gather.12.cloned.1.call-done
  226.9 2.3 fusion.47
  229.2 57.6 %all-gather.8.cloned.1.call-done = bf16[2048,1024]{0,1:T(8,128)(2,1)} async-done(((bf16[128,1024]{0,1:T(8,128)(2,1)}), bf16[2048,1024]{0,1:T(8,128)(2,1)}) %all-gather.8.cloned.1.call-update) | async-done | bytes 4194320 | tf_op jit(solution)/shard_map/all_gather | solution.py:92
  286.9 4.7 fusion.46
  291.6 3.3 pad_maximum_fusion
  294.9 0.0 all-gather.14.cloned.1.call-start
  295.0 0.9 copy-done.3
  295.8 0.1 copy.20
  296.0 0.1 copy.13
  296.1 127.9 %reduce-scatter.3.cloned.1.call-done = f32[256,768]{0,1:T(8,128)} async-done(((f32[2048,768]{0,1:T(8,128)}), f32[256,768]{0,1:T(8,128)}) %reduce-scatter.3.cloned.1.call-update) | async-done | bytes 786448 | tf_op jit(solution)/shard_map/reduce_scatter | solution.py:103
  424.0 1.1 multiply_reduce_fusion
  425.1 1.0 multiply_reduce_fusion.1
  426.1 37.3 %all-reduce = (f32[256]{0:T(256)S(1)}, f32[256]{0:T(256)S(1)}) all-reduce(f32[256]{0:T(256)S(1)} %multiply_reduce_fusion.1, f32[256]{0:T(256)S(1)} %multiply_reduce_fusion), channel_id=1, replica_groups=mesh['seq'=16,'tp'=8] {'seq'}, use_global_device_ids=true, to_apply=%region_6.7 | all-reduce | flops 512 | bytes 4096 | tf_op jit(solution)/shard_map/psum | solution.py:106
  463.4 1.7 multiply_convert_fusion
  465.1 0.3 reduce-scatter.5.cloned.1.call-start
  465.4 45.0 %all-gather.14.cloned.1.call-done = bf16[256,4096]{0,1:T(8,128)(2,1)} async-done(((bf16[256,256]{0,1:T(8,128)(2,1)}), bf16[256,4096]{0,1:T(8,128)(2,1)}) %all-gather.14.cloned.1.call-update) | async-done | bytes 2097168 | tf_op jit(solution)/shard_map/all_gather | solution.py:117
  510.4 4.8 fusion.20
  515.3 5.7 fusion.48
  521.0 168.2 %reduce-scatter.5.cloned.1.call-done = f32[512,512]{1,0:T(8,128)} async-done(((f32[4096,512]{1,0:T(8,128)}), f32[512,512]{1,0:T(8,128)}) %reduce-scatter.5.cloned.1.call-update) | async-done | bytes 1048592 | tf_op jit(solution)/shard_map/reduce_scatter | solution.py:121
  (29 shorter events, 0.2 us)
Async XLA Ops:
  6.5 280.3 %copy-start = (bf16[1024,512]{1,0:T(8,128)(2,1)S(1)}, bf16[1024,512]{1,0:T(8,128)(2,1)}, u32[]{:S(2)}) copy-start(bf16[1024,512]{1,0:T(8,128)(2,1)} %param.18) | copy-start | bytes 3145732
  6.5 70.0 %all-gather.6.cloned.1.call-start = ((), (), s32[]{:S(2)}) async-start(), calls=%async_computation.2 | async-start | bytes 6684672 | tf_op jit(solution)/shard_map/all_gather | solution.py:80
  7.3 134.4 %all-gather.10.cloned.1.call-start = ((), (), s32[]{:S(2)}) async-start(), calls=%async_computation.4 | async-start | bytes 6684672 | tf_op jit(solution)/shard_map/all_gather | solution.py:87
  8.0 218.9 %all-gather.12.cloned.1.call-start = ((), (), s32[]{:S(2)}) async-start(), calls=%async_computation.5 | async-start | bytes 2228224 | tf_op jit(solution)/shard_map/all_gather | solution.py:93
  15.1 126.5 %copy-start.6 = (bf16[128,512]{1,0:T(8,128)(2,1)S(1)}, bf16[128,512]{1,0:T(8,128)(2,1)}, u32[]{:S(2)}) copy-start(bf16[128,512]{1,0:T(8,128)(2,1)} %param.14) | copy-start | bytes 393220
  178.8 108.1 %all-gather.8.cloned.1.call-start = ((), (), s32[]{:S(2)}) async-start(), calls=%async_computation.3 | async-start | bytes 4456448 | tf_op jit(solution)/shard_map/all_gather | solution.py:92
  200.5 26.4 %copy-start.2 = (bf16[512,256]{1,0:T(8,128)(2,1)S(1)}, bf16[512,256]{1,0:T(8,128)(2,1)}, u32[]{:S(2)}) copy-start(bf16[512,256]{1,0:T(8,128)(2,1)} %param.21) | copy-start | bytes 786436
  221.9 202.0 %reduce-scatter.3.cloned.1.call-start = ((), (), s32[]{:S(2)}) async-start(), calls=%async_computation.6 | async-start | bytes 7077888 | tf_op jit(solution)/shard_map/reduce_scatter | solution.py:103
  294.9 0.9 copy-start.3
  294.9 1.1 copy-start.4
  294.9 168.5 %copy-start.5 = (f32[256]{0:T(256)S(1)}, f32[256]{0:T(256)}, u32[]{:S(2)}) copy-start(f32[256]{0:T(256)} %param.22) | copy-start | bytes 3076
  294.9 215.5 %copy-start.7 = (f32[512]{0:T(512)S(1)}, f32[512]{0:T(512)}, u32[]{:S(2)}) copy-start(f32[512]{0:T(512)} %param.19) | copy-start | bytes 6148
  294.9 215.5 %all-gather.14.cloned.1.call-start = ((), (), s32[]{:S(2)}) async-start(), calls=%async_computation.7 | async-start | bytes 2228224 | tf_op jit(solution)/shard_map/all_gather | solution.py:117
  465.1 224.1 %reduce-scatter.5.cloned.1.call-start = ((), (), s32[]{:S(2)}) async-start(), calls=%async_computation.8 | async-start | bytes 9437184 | tf_op jit(solution)/shard_map/reduce_scatter | solution.py:121
  510.4 4.8 copy-start.1
Sparse Core Ops, SparseCore 0:
  9.8 66.6 all-gather.5
  79.0 62.5 all-gather.9
  178.9 47.9 all-gather.11
  229.0 57.8 all-gather.7
  295.1 128.8 reduce-scatter.2
  465.3 45.0 all-gather.13
  521.1 168.0 reduce-scatter.4
where the time goes:
time: 697 us; the launch traced here: 696 us
  waiting for transfers between devices  510 us (73%)
  matrix products  86.2 us (12%)
  other arithmetic  46.5 us (7%)
  blocking collectives  37.3 us (5%)
  between operations  14.3 us (2%)
    reduce_scatter x1, waiting for transfers between devices, per_device(): lax.psum_scatter(lax.dot_general(wide_normed, delta, (((0,), (0,)), ((),...  168 us
    reduce_scatter x1, waiting for transfers between devices, per_device(): lax.psum_scatter(partial_sums, 'tp', scatter_dimension=0, tiled=True)  128 us
    all_gather x1, waiting for transfers between devices, per_device(): lax.all_gather(teacher_kv, 'seq', axis=1, tiled=True)  61.4 us
    all_gather x1, waiting for transfers between devices, per_device(): lax.all_gather(teacher_context, 'seq', axis=0, tiled=True)  57.6 us
    all_gather x1, waiting for transfers between devices, per_device(): full_normed = lax.all_gather(normed, 'seq', axis=1, tiled=True)  45 us
    all_gather x1, waiting for transfers between devices, per_device(): lax.all_gather(student_kv, 'seq', axis=1, tiled=True)  43.6 us
    psum x1, blocking collectives, per_device(): lax.psum((jnp.sum(teacher_hidden * teacher_hidden, axis=1), jnp.sum(stude...  37.3 us
    dot_general x2, matrix products, fold_piece(): jnp.einsum('tkgn,nkd->tkgd', weights.astype(jnp.bfloat16), values_piece,...  34.4 us
  transfers between devices with their start and end apart: 7, of which 7 were waited for; matrix products, arithmetic and copies ran while one was open for 11% of the time, Pallas kernels for 0%

commit v1 on v0

v1 whole, which is shorter than its diff:
```python
import math

import jax
import jax.numpy as jnp
from jax import lax
from jax.experimental import pallas as pl
from jax.experimental.pallas import tpu as pltpu
from jax.sharding import PartitionSpec as P

D_T = 8192
D_S = 4096
HEAD = 128
SLAB = 2048
CACHE = 10240
KEYS_CHIP = 1536
HIDDEN = -1e30
LOG2E = math.log2(math.e)
SCALE = LOG2E / math.sqrt(HEAD)
MESH = pl.DeviceIdType.MESH
BF = jnp.bfloat16
F32 = jnp.float32


class Wire:
    def __init__(self, send, recv):
        self.send, self.recv, self.made = send, recv, []

    def copy(self, src, dst, dev):
        i = len(self.made)
        made = pltpu.make_async_remote_copy(
            src_ref=src, dst_ref=dst, send_sem=self.send.at[i], recv_sem=self.recv.at[i],
            device_id=dev, device_id_type=MESH,
        )
        self.made.append(made)
        return made

    def close(self):
        for made in self.made:
            made.wait_send()


class Gather:
    def __init__(self, wire, block, right, left, across=None, core=None, planes=None):
        self.planes = planes or (1 if across is None else 2)
        self.core = core is not None
        self.cross = wire.copy(block(0, 0, None), block(0, 0, None), across) if across is not None else None
        self.right, self.left, self.on_right, self.on_left, self.pass_on = [], [], [], [], []
        for plane in range(self.planes):
            own = block(plane, 0, None)
            self.right.append(wire.copy(own, own, right))
            self.left.append(wire.copy(own, own, left))
            first, second = block(plane, 3, 0), block(plane, 1, 1)
            self.on_right.append(wire.copy(first, first, right))
            self.on_left.append(wire.copy(second, second, left))
            if self.core:
                refs = [own, block(plane, 3, None), block(plane, 1, None), block(plane, 2, 0), block(plane, 2, 1)]
                self.pass_on.append([wire.copy(ref, ref, core) for ref in refs])

    def root(self, plane):
        if plane == 1 and self.cross is not None:
            self.cross.wait_recv()
        self.right[plane].start()
        self.left[plane].start()
        if plane == 0 and self.cross is not None:
            self.cross.start()
        if self.core:
            self.pass_on[plane][0].start()

    def mid(self, plane):
        self.right[plane].wait_recv()
        self.on_right[plane].start()
        if self.core:
            self.pass_on[plane][1].start()
        self.left[plane].wait_recv()
        self.on_left[plane].start()
        if self.core:
            self.pass_on[plane][2].start()

    def far(self, plane):
        self.on_right[plane].wait_recv()
        if self.core:
            self.pass_on[plane][3].start()
        self.on_left[plane].wait_recv()
        if self.core:
            self.pass_on[plane][4].start()

    def have_own(self, plane):
        self.pass_on[plane][0].wait_recv()

    def have_left(self, plane):
        self.pass_on[plane][1].wait_recv()

    def have_right(self, plane):
        self.pass_on[plane][2].wait_recv()

    def have_near(self, plane):
        self.have_left(plane)
        self.have_right(plane)

    def have_far(self, plane):
        self.pass_on[plane][3].wait_recv()
        self.pass_on[plane][4].wait_recv()


def dot(a, b, dims=((1,), (0,)), precision=None):
    return lax.dot_general(a, b, (dims, ((), ())), precision=precision, preferred_element_type=F32)


def scratch_plan():
    V = pltpu.VMEM
    D = pltpu.SemaphoreType.DMA
    return dict(
        kv=V((2, 4, 2, 2, 768, 128), BF),
        kx=V((2, 4, 2, 768, 256), BF),
        vt=V((2, 4, 2, 144, 768), BF),
        qa=V((3, 2, 512, 256), BF),
        tq_in=V((128, 1024), BF),
        sq_in=V((128, 512), BF),
        m=V((3, 2, 8, 512), F32),
        acc=V((3, 2, 144, 512), F32),
        o_out=V((3, 2, 128, 512), BF),
        o_in=V((3, 2, 128, 512), BF),
        l_out=V((3, 2, 8, 512), F32),
        l_in=V((3, 2, 8, 512), F32),
        tctx=V((8, 2, 128, 1024), BF),
        sctx=V((8, 2, 128, 512), BF),
        tw=V((1024, 512), BF),
        sw=V((512, 256), BF),
        mp=V((8, 512, 512), BF),
        ty_out=V((2, 128, 512), BF),
        ty_in=V((2, 128, 512), BF),
        sy_out=V((256, 256), BF),
        sy_in=V((256, 256), BF),
        tpart=V((2, 4, 2, 128, 512), F32),
        spart=V((4, 2, 256, 256), F32),
        tr_out=V((2, 2, 128, 512), BF),
        tr_in=V((2, 2, 2, 64, 512), BF),
        sr_out=V((2, 256, 256), BF),
        sr_in=V((2, 2, 128, 256), BF),
        tz_out=V((2, 2, 2, 128, 512), BF),
        tz_in=V((2, 2, 2, 128, 512), BF),
        sz_out=V((2, 2, 256, 256), BF),
        sz_in=V((2, 2, 256, 256), BF),
        thid=V((2, 128, 512), F32),
        shid=V((256, 256), F32),
        tsq=V((2, 16, 8, 128), F32),
        ssq=V((16, 8, 256), F32),
        nb=V((16, 256, 256), BF),
        ng=V((8, 2, 256, 256), BF),
        dl=V((2, 8, 128, 512), BF),
        diff=V((2, 128, 512), F32),
        wsend=D((200,)),
        wrecv=D((200,)),
        loc=D((8,)),
    )


def kernel(doc, tq, tkv_h, sq, skv_h, tres, tw_h, tg, sres, sw_h, sg, mp_h, out, *scratch):
    b = dict(zip(scratch_plan(), scratch))
    s = lax.axis_index("seq")
    p = lax.axis_index("tp")
    yh, x, c = s // 8, (s // 2) % 4, s % 2
    z, yl = p // 2, p % 2
    k_own = yh * 4 + x

    def seq_dev(plane, off, other):
        return ((((yh + plane) % 2) * 4 + (x + off) % 4) * 2 + (c + other) % 2, p)

    def tp_dev(plane, off):
        return (s, ((z + off) % 4) * 2 + (yl + plane) % 2)

    right, left, across, core = seq_dev(0, 1, 0), seq_dev(0, 3, 0), seq_dev(1, 0, 0), seq_dev(0, 0, 1)

    loads = [
        pltpu.make_async_copy(skv_h, b["kv"].at[0, x, c], b["loc"].at[0]),
        pltpu.make_async_copy(tkv_h, b["kv"].at[1, x, c], b["loc"].at[1]),
        pltpu.make_async_copy(sw_h, b["sw"], b["loc"].at[2]),
        pltpu.make_async_copy(tw_h, b["tw"], b["loc"].at[3]),
        pltpu.make_async_copy(mp_h, b["mp"], b["loc"].at[4]),
    ]
    for load in loads:
        load.start()

    barrier = pltpu.get_barrier_semaphore()
    for off in range(1, 16):
        pl.semaphore_signal(barrier, inc=1, device_id=((s + off) % 16, p), device_id_type=MESH)
    for off in range(1, 8):
        pl.semaphore_signal(barrier, inc=1, device_id=(s, (p + off) % 8), device_id_type=MESH)
    pl.semaphore_wait(barrier, 22)

    wire = Wire(b["wsend"], b["wrecv"])
    give_sq = wire.copy(sq, b["sq_in"], across)
    give_tq = wire.copy(tq, b["tq_in"], across)

    def kv_block(model):
        def block(plane, off, part):
            at = (x + off) % 4
            if part is None:
                return b["kv"].at[model, at, c]
            return b["kv"].at[model, at, c, part]

        return block

    def s_block(plane, off, part):
        at = ((yh + plane) % 2) * 4 + (x + off) % 4
        if part is None:
            return b["sctx"].at[at, c]
        return b["sctx"].at[at, c, pl.ds(part * 64, 64)]

    def t_block(half):
        def block(plane, off, part):
            at = ((yh + plane) % 2) * 4 + (x + off) % 4
            if part is None:
                return b["tctx"].at[at, c, pl.ds(half * 64, 64)]
            return b["tctx"].at[at, c, pl.ds(half * 64 + part * 32, 32)]

        return block

    def nb_block(plane, off, part):
        at = (((yh + plane) % 2) * 4 + (x + off) % 4) * 2 + c
        if part is None:
            return b["nb"].at[at]
        return b["nb"].at[at, pl.ds(part * 128, 128)]

    def dl_block(half):
        def block(plane, off, part):
            at = ((z + off) % 4) * 2 + (yl + plane) % 2
            if part is None:
                return b["dl"].at[half, at]
            return b["dl"].at[half, at, pl.ds(part * 64, 64)]

        return block

    g_skv = Gather(wire, kv_block(0), right, left, None, core)
    g_tkv = Gather(wire, kv_block(1), right, left, None, core)
    g_s = Gather(wire, s_block, right, left, None, core, 2)
    g_t = [Gather(wire, t_block(half), right, left, None, core, 2) for half in range(2)]
    g_n = Gather(wire, nb_block, right, left, across, core)
    g_d = [Gather(wire, dl_block(half), tp_dev(0, 1), tp_dev(0, 3), tp_dev(1, 0), None) for half in range(2)]
    give_o = [[wire.copy(b["o_out"].at[i, 1 - g], b["o_in"].at[i, g], across) for g in range(2)] for i in range(3)]
    give_l = [[wire.copy(b["l_out"].at[i, 1 - g], b["l_in"].at[i, g], across) for g in range(2)] for i in range(3)]
    s_sq = [wire.copy(b["ssq"].at[s], b["ssq"].at[s], ((s + off) % 16, p)) for off in range(1, 16)]
    t_sq = [
        [wire.copy(b["tsq"].at[half, s], b["tsq"].at[half, s], ((s + off) % 16, p)) for off in range(1, 16)]
        for half in range(2)
    ]
    n_tp = [
        wire.copy(b["nb"].at[((p + off) % 8) * 2 + c], b["ng"].at[p, c], (s, (p + off) % 8)) for off in range(1, 8)
    ]
    n_core = [
        wire.copy(b["ng"].at[(p + 8 - off) % 8, c], b["ng"].at[(p + 8 - off) % 8, c], core) for off in range(1, 8)
    ]

    qa, m, acc = b["qa"], b["m"], b["acc"]
    heads, tokens = (4, 8, 8), (128, 64, 64)

    def fill_queries(one, src, group):
        first = 64 * (one // 2)
        for h in range(heads[one]):
            rows = slice(h * tokens[one], (h + 1) * tokens[one])
            qa[one, group, rows, 0:128] = src[first : first + tokens[one], h * 128 : (h + 1) * 128]

    def prepare(model, passes):
        rows = lax.broadcasted_iota(jnp.int32, (128, 128), 0)
        lanes = lax.broadcasted_iota(jnp.int32, (128, 128), 1)
        for one in passes:
            eye = jnp.where(rows % tokens[one] + 64 * (one // 2) == lanes, 1.0, 0.0).astype(BF)
            for g in range(2):
                for i in range(4):
                    qa[one, g, i * 128 : (i + 1) * 128, 128:256] = eye
            m[one] = jnp.full((2, 8, 512), HIDDEN, F32)
            acc[one] = jnp.zeros((2, 144, 512), F32)

        def extra(i, carry):
            b["kx"][model, i, :, :, 128:256] = jnp.zeros((2, 768, 128), BF)
            b["vt"][model, i, :, 128:144, :] = jnp.ones((2, 16, 768), BF)
            return carry

        lax.fori_loop(0, 4, extra, 0)

    first_key = doc[0]

    def attention(hooks):
        def step(n, carry):
            for at_step, hook in hooks.items():
                pl.when(n == at_step)(hook)
            one, i, half, g = n // 16, (n % 16) // 4, (n % 4) // 2, n % 2
            model = (one + 1) // 2
            at = (x + 3 * i + 3 * (i // 2) + 2 * (i // 3)) % 4
            from_core = (c + half) % 2
            base = (yh * 4 + at) * KEYS_CHIP + from_core * 768

            @pl.when((g == 0) & (one <= 1))
            def _():
                b["vt"][model, at, from_core, 0:128, :] = b["kv"][model, at, from_core, 1].T
                b["kx"][model, at, from_core, :, 0:128] = b["kv"][model, at, from_core, 0]

            @pl.when((yh == 0) & (g == 0) & (one <= 1))
            def _():
                key = lax.broadcasted_iota(jnp.int32, (768, 128), 0)
                b["kx"][model, at, from_core, :, 128:256] = jnp.where(key >= first_key - base, 0.0, HIDDEN).astype(BF)

            @pl.when((yh == 1) & (at >= 2))
            def _():
                first_row = CACHE + ((((yh + g) % 2) * 4 + x) * 2 + c) * 128
                key = lax.broadcasted_iota(jnp.int32, (768, 128), 0)
                row = lax.broadcasted_iota(jnp.int32, (768, 128), 1)
                b["kx"][model, at, from_core, :, 128:256] = jnp.where(key - row <= first_row - base, 0.0, HIDDEN).astype(BF)

            scores = dot(b["kx"][model, at, from_core], qa[one, g], ((1,), (1,)))
            old = m[one, g]
            new = jnp.maximum(old, jnp.broadcast_to(jnp.max(scores, axis=0, keepdims=True), (8, 512)))
            weights = jnp.exp2((scores.reshape(96, 8, 512) - new[None]) * SCALE).reshape(768, 512).astype(BF)
            shrink = jnp.exp2((old - new) * SCALE)
            fresh = dot(b["vt"][model, at, from_core], weights)
            m[one, g] = new
            acc[one, g] = (acc[one, g].reshape(18, 8, 512) * shrink[None]).reshape(144, 512) + fresh
            return carry

        lax.fori_loop(0, 48, step, 0)

    def part_of(one, g):
        total = acc[one, g, 128:136, :]
        mean = (acc[one, g, 0:128, :].reshape(16, 8, 512) * (1.0 / total)[None]).reshape(128, 512)
        return mean, m[one, g] * SCALE + jnp.log(total) * LOG2E

    def partner_part(one):
        for g in (1, 0):
            mean, logs = part_of(one, g)
            b["o_out"][one, g] = mean.astype(BF)
            b["l_out"][one, g] = logs
            give_o[one][1 - g].start()
            give_l[one][1 - g].start()

    def combine(one, g, ctx):
        give_o[one][g].wait_recv()
        give_l[one][g].wait_recv()
        mine, log_mine = part_of(one, g)
        share = 1.0 / (1.0 + jnp.exp2(log_mine - b["l_in"][one, g]))
        other = b["o_in"][one, g].astype(F32)
        both = mine + ((other - mine).reshape(16, 8, 512) * share[None]).reshape(128, 512)
        both = both.T.astype(BF)
        count, first = tokens[one], 64 * (one // 2)
        for h in range(heads[one]):
            held = both[h * count : (h + 1) * count, :]
            ctx[((yh + g) % 2) * 4 + x, c, first : first + count, h * 128 : (h + 1) * 128] = held

    class Reduce:
        def __init__(self, ctx, w, name, half):
            self.ctx, self.w, self.half = ctx, w, half

            def of(key):
                return b[name + key] if half is None else b[name + key].at[half]

            self.y_out, self.y_in, self.part, self.hid = of("y_out"), of("y_in"), of("part"), of("hid")
            self.r_out, self.r_in, self.z_out, self.z_in = of("r_out"), of("r_in"), of("z_out"), of("z_in")
            self.rows = self.part.shape[2] // 2
            near = (tp_dev(0, 3), tp_dev(0, 1))
            self.relay = [
                wire.copy(self.r_out.at[:, pl.ds(i * self.rows, self.rows)], self.r_in.at[i], near[i]) for i in range(2)
            ]
            self.along = [wire.copy(self.z_out.at[i], self.z_in.at[i], near[i]) for i in range(2)]
            self.beside = wire.copy(self.y_out, self.y_in, tp_dev(1, 0))

        def multiply(self, first, last, waits):
            def pair(j, carry):
                for at, wait in waits.items():
                    pl.when(j == at)(wait)
                zd = ((yh + j // 2) % 2) * 2 + (x // 2 + j % 2) % 2

                both = pl.ds(zd * 2, 2)
                if self.half is None:
                    held = self.ctx[both]
                else:
                    held = self.ctx[both, :, self.half * 64 : self.half * 64 + 64]
                done = dot(held.reshape(-1, held.shape[3]), self.w[...])
                self.part[zd] = done.reshape(2, -1, done.shape[1])

                @pl.when(zd == (z + 2) % 4)
                def _():
                    self.r_out[...] = self.part[zd].astype(BF)
                    self.relay[0].start()
                    self.relay[1].start()

                return carry

            lax.fori_loop(first, last, pair, 0)

        def send_on(self):
            for i, zd in enumerate(((z + 3) % 4, (z + 1) % 4)):
                mid = slice(i * self.rows, (i + 1) * self.rows)
                rest = slice((1 - i) * self.rows, (2 - i) * self.rows)
                self.z_out[i, :, rest, :] = self.part[zd, :, rest, :].astype(BF)
                self.relay[i].wait_recv()
                self.z_out[i, :, mid, :] = (self.part[zd, :, mid, :] + self.r_in[i].astype(F32)).astype(BF)
                self.along[i].start()

        def settle(self):
            self.along[0].wait_recv()
            self.along[1].wait_recv()

            def block(u):
                return self.part[z, u] + self.z_in[0, u].astype(F32) + self.z_in[1, u].astype(F32)

            self.y_out[...] = block(1 - yl).astype(BF)
            self.beside.start()
            self.hid[...] = block(yl)

        def finish(self, resid):
            if self.half is None:
                own = resid[...]
            else:
                first = self.half * 64
                own = jnp.concatenate([resid[first : first + 64, :], resid[first + 128 : first + 192, :]], axis=0)
            total = self.hid[...] + own.astype(F32)
            self.beside.wait_recv()
            self.hid[...] = total + self.y_in[...].astype(F32)

    def send_squares(hid, sq, copies):
        value = hid[...]
        ones = jnp.ones((8, value.shape[1]), F32)
        sq[s] = dot(ones, value * value, ((1,), (1,)), lax.Precision.HIGHEST)
        for made in copies:
            made.start()

    def inverse_scale(sq, copies, width):
        for made in copies:
            made.wait_recv()
        total = sq[0]
        for i in range(1, 16):
            total = total + sq[i]
        first = jnp.where(lax.broadcasted_iota(jnp.int32, (8, 128), 0) == 0, 1.0, 0.0)
        column = dot(total, first, ((0,), (0,)), lax.Precision.HIGHEST)
        return 1.0 / jnp.sqrt(column * (1.0 / width) + 1e-05)

    r_s = Reduce(b["sctx"], b["sw"], "s", None)
    r_t = [Reduce(b["tctx"], b["tw"], "t", half) for half in range(2)]

    def ready(gather, plane):
        gather.have_own(plane)
        gather.have_near(plane)
        gather.have_far(plane)

    give_sq.start()
    loads[0].wait()
    g_skv.root(0)
    give_tq.start()
    fill_queries(0, sq, 0)
    prepare(0, (0,))

    def s_partner():
        give_sq.wait_recv()
        fill_queries(0, b["sq_in"], 1)

    def s_near():
        prepare(1, (1, 2))
        fill_queries(1, tq, 0)
        fill_queries(2, tq, 0)
        loads[1].wait()
        g_skv.mid(0)
        g_tkv.root(0)

    def t_start():
        partner_part(0)
        give_tq.wait_recv()
        fill_queries(1, b["tq_in"], 1)
        fill_queries(2, b["tq_in"], 1)

    def t_near():
        g_tkv.mid(0)
        g_tkv.have_own(0)

    def context(one, g, ctx, gather):
        combine(one, g, ctx)
        gather.root(g)

    def s_sums():
        for load in loads[2:]:
            load.wait()
        r_s.multiply(0, 4, {0: lambda: ready(g_s, 0), 2: lambda: ready(g_s, 1)})

    def s_squares():
        r_s.finish(sres)
        send_squares(b["shid"], b["ssq"], s_sq)

    def s_normed():
        inverse = inverse_scale(b["ssq"], s_sq, D_S)
        inverse = jnp.concatenate([inverse, inverse], axis=1)
        normed = (b["shid"][...] * inverse * sg[...]).astype(BF)
        for at, first in enumerate((0, 128, 64, 192)):
            b["nb"][s, at * 64 : (at + 1) * 64, :] = normed[first : first + 64, :]
        g_n.root(0)

    def t1_sums():
        r_t[0].multiply(0, 4, {0: lambda: ready(g_t[0], 0), 2: lambda: ready(g_t[0], 1)})

    def s_last_spread():
        g_s.mid(1)
        g_s.far(0)

    def s_squares_t1():
        s_squares()
        g_t[0].mid(0)

    def t1_spread():
        g_t[0].mid(1)
        g_t[0].far(0)

    def last():
        g_n.mid(0)
        t1_sums()

    attention(
        {
            1: s_partner,
            2: lambda: g_skv.have_own(0),
            4: s_near,
            6: lambda: g_skv.have_left(0),
            10: lambda: g_skv.have_right(0),
            12: lambda: g_skv.far(0),
            14: lambda: g_skv.have_far(0),
            16: t_start,
            18: t_near,
            21: lambda: context(0, 0, b["sctx"], g_s),
            22: lambda: g_tkv.have_left(0),
            25: lambda: context(0, 1, b["sctx"], g_s),
            26: lambda: g_tkv.have_right(0),
            27: lambda: g_s.mid(0),
            28: lambda: g_tkv.far(0),
            29: s_last_spread,
            30: lambda: g_tkv.have_far(0),
            31: lambda: g_s.far(1),
            32: lambda: partner_part(1),
            33: s_sums,
            35: r_s.send_on,
            37: lambda: context(1, 0, b["tctx"], g_t[0]),
            39: r_s.settle,
            41: lambda: context(1, 1, b["tctx"], g_t[0]),
            42: s_squares_t1,
            44: s_normed,
            45: t1_spread,
            46: lambda: g_t[0].far(1),
            47: last,
        }
    )
    partner_part(2)
    g_n.root(1)
    r_t[0].send_on()
    g_n.far(0)
    g_n.mid(1)
    context(2, 0, b["tctx"], g_t[1])
    g_n.far(1)
    r_t[0].settle()
    for made in n_tp:
        made.start()
    ready(g_n, 0)
    ready(g_n, 1)
    b["diff"][...] = jnp.zeros((2, 128, 512), F32)

    def match(k, carry):
        lhs = jnp.concatenate([b["nb"][2 * k], b["nb"][2 * k + 1]], axis=1)
        b["diff"][...] += dot(lhs, b["mp"][k]).reshape(2, 128, 512)
        return carry

    lax.fori_loop(0, 8, match, 0)

    def delta(half):
        inverse = inverse_scale(b["tsq"].at[half], t_sq[half], D_T)
        inverse = jnp.concatenate([inverse, inverse, inverse, inverse], axis=1)
        target = b["thid"][half] * inverse * tg[...]
        b["dl"][half, p] = ((b["diff"][half] - target) * (1.0 / math.sqrt(SLAB))).astype(BF)
        g_d[half].root(0)

    def gradient(half, plane, offs):
        def one(i, carry):
            q = ((z + offs[0] + i * offs[1]) % 4) * 2 + (yl + plane) % 2
            for at in range(2):
                rows = slice(at * 256, (at + 1) * 256)
                lhs = b["ng"][q, at, half * 128 : (half + 1) * 128, :]
                out[rows, :] += dot(lhs, b["dl"][half, q], ((0,), (0,)))
            return carry

        lax.fori_loop(0, offs[2], one, 0)

    own, near, far = (0, 1, 1), (1, 2, 2), (2, 1, 1)
    context(2, 1, b["tctx"], g_t[1])
    g_t[1].mid(0)
    g_t[1].far(0)
    r_t[0].finish(tres)
    send_squares(b["thid"].at[0], b["tsq"].at[0], t_sq[0])
    r_t[1].multiply(0, 2, {0: lambda: ready(g_t[1], 0)})
    g_t[1].mid(1)
    g_t[1].far(1)
    delta(0)
    r_t[1].multiply(2, 4, {2: lambda: ready(g_t[1], 1)})
    for made, onward in zip(n_tp, n_core):
        made.wait_recv()
        onward.start()
    b["ng"][p, 0] = b["nb"][2 * p]
    b["ng"][p, 1] = b["nb"][2 * p + 1]
    out[...] = jnp.zeros((512, 512), F32)
    r_t[1].send_on()
    g_d[0].mid(0)
    g_d[0].root(1)
    for made in n_core:
        made.wait_recv()
    gradient(0, 0, own)
    gradient(0, 0, near)
    r_t[1].settle()
    g_d[0].far(0)
    g_d[0].mid(1)
    r_t[1].finish(tres)
    send_squares(b["thid"].at[1], b["tsq"].at[1], t_sq[1])
    gradient(0, 0, far)
    gradient(0, 1, own)
    delta(1)
    gradient(0, 1, near)
    g_d[0].far(1)
    gradient(0, 1, far)
    gradient(1, 0, own)
    g_d[1].mid(0)
    g_d[1].root(1)
    gradient(1, 0, near)
    gradient(1, 1, own)
    g_d[1].far(0)
    g_d[1].mid(1)
    gradient(1, 0, far)
    gradient(1, 1, near)
    g_d[1].far(1)
    gradient(1, 1, far)
    wire.close()


def per_device(tq, tkv, sq, skv, doc, tres, tw, tg, sres, sw, sg, mp):
    V = pl.BlockSpec(memory_space=pltpu.VMEM)
    A = pl.BlockSpec(memory_space=pl.ANY)
    S = pl.BlockSpec(memory_space=pltpu.SMEM)
    return pl.pallas_call(
        kernel,
        out_shape=jax.ShapeDtypeStruct((512, 512), F32),
        in_specs=[S, V, A, V, A, V, A, V, V, A, V, A],
        out_specs=V,
        scratch_shapes=list(scratch_plan().values()),
        compiler_params=pltpu.CompilerParams(
            collective_id=0, has_side_effects=True, vmem_limit_bytes=63 * 1024 * 1024
        ),
    )(
        doc, tq, tkv, sq, skv, tres, tw, tg.reshape(1, -1), sres, sw, sg.reshape(1, -1), mp.reshape(8, 512, 512)
    )


def solution(mesh):
    in_specs = (
        P("seq", "tp"),
        P(None, "seq", "tp"),
        P("seq", "tp"),
        P(None, "seq", "tp"),
        P(),
        P("tp", "seq"),
        P("tp", "seq"),
        P("seq"),
        P("tp", "seq"),
        P("tp", "seq"),
        P("seq"),
        P(None, "seq"),
    )
    out_specs = P("tp", "seq")
    return jax.shard_map(per_device, mesh=mesh, in_specs=in_specs, out_specs=out_specs, check_vma=False)
```

time: 697 us -> 168 us (0.24)
  waiting for transfers between devices: 510 us -> 0 us
  Pallas kernels: 0 us -> 165 us
  matrix products: 86.2 us -> 0 us
  other arithmetic: 46.5 us -> 0 us
  blocking collectives: 37.3 us -> 0 us
  between operations: 14.3 us -> 0.66 us
    reduce_scatter x2 -> x0, waiting for transfers between devices: 296 us -> none  [the longest x1 168 us: per_device(): lax.psum_scatter(lax.dot_general(wide_normed, delta, (((0,), (0,)), ((),...]
    all_gather x5 -> x0, waiting for transfers between devices: 213 us -> none  [the longest x1 61.4 us: per_device(): lax.all_gather(teacher_kv, 'seq', axis=1, tiled=True)]
    pallas_call x0 -> x1, Pallas kernels: none -> 165 us  [per_device(): pl.pallas_call(kernel, out_shape=jax.ShapeDtypeStruct((512, 512), F32), i...]
    dot_general x8 -> x0, matrix products: 86.2 us -> none  [the longest x2 34.4 us: fold_piece(): jnp.einsum('tkgn,nkd->tkgd', weights.astype(jnp.bfloat16), values_piece,...]
    psum x1 -> x0, blocking collectives: 37.3 us -> none  [per_device(): lax.psum((jnp.sum(teacher_hidden * teacher_hidden, axis=1), jnp.sum(stude...]
    reduce_sum x4 -> x0, other arithmetic: 35.1 us -> none  [the longest x2 32.9 us: fold_piece(): total = jnp.sum(weights, axis=-1)]
  transfers between devices with their start and end apart: 7 -> 0, of which waited for: 7 -> 0; matrix products, arithmetic and copies ran while one was open for 11% -> 0% of each run, Pallas kernels for 0% -> 0%
where the time goes in v1:
time: 168 us
  Pallas kernels  165 us (98%)
  local copies, waits for them, and re-layouts  2.26 us (1%)
    pallas_call x1, Pallas kernels, per_device(): pl.pallas_call(kernel, out_shape=jax.ShapeDtypeStruct((512, 512), F32), i...  165 us

profile of v1, /device:TPU:0, one launch (start us, length us, event | category | flops | bytes accessed | tf_op | source)
XLA Modules:
  0.0 167.6 jit_solution(11549854408987273924)
XLA Ops:
  0.7 164.7 %shard_map.118 = f32[512,512]{1,0:T(8,128)} custom-call(s32[1]{0:T(128)S(6)} %copy.14.doc, bf16[128,1024]{1,0:T(8,128)(2,1)} %tq.1, bf16[2,768,128]{2,1,0:T(8,128)(2,1)} %tkv_h.1, bf16[128,512]{1,0:T(8,128)(2,1)} %sq.1, bf16[2,768,128]{2,1,0:T(8,128)(2,1)} %skv_h.1, bf16[256,512]{1,0:T(8,128)(2,1)} %tres.1, bf16[1024,512]{1,0:T(8,128)(2,1)} %tw_h.1, ...), custom_call_target="tpu_custom_call" | custom-call | tf_op jit(solution)/shard_map/pallas_call | solution.py:638
  165.3 2.3 %copy.15 = f32[512,512]{1,0:T(8,128)} copy(f32[512,512]{1,0:T(8,128)} %shard_map.118) | data formatting | bytes 2097152

commit v2 on v1

--- a/solution.py
+++ b/solution.py
@@ -23,7 +23,7 @@
 
 class Wire:
     def __init__(self, send, recv):
-        self.send, self.recv, self.made = send, recv, []
+        self.send, self.recv, self.made, self.left = send, recv, [], set()
 
     def copy(self, src, dst, dev):
         i = len(self.made)
@@ -34,9 +34,11 @@
         self.made.append(made)
         return made
 
-    def close(self):
-        for made in self.made:
-            made.wait_send()
+    def close(self, first=0, last=None):
+        for i in range(first, len(self.made) if last is None else last):
+            if i not in self.left:
+                self.left.add(i)
+                self.made[i].wait_send()
 
 
 class Gather:
@@ -56,12 +58,12 @@
                 refs = [own, block(plane, 3, None), block(plane, 1, None), block(plane, 2, 0), block(plane, 2, 1)]
                 self.pass_on.append([wire.copy(ref, ref, core) for ref in refs])
 
-    def root(self, plane):
+    def root(self, plane, start_cross=True):
         if plane == 1 and self.cross is not None:
             self.cross.wait_recv()
         self.right[plane].start()
         self.left[plane].start()
-        if plane == 0 and self.cross is not None:
+        if plane == 0 and self.cross is not None and start_cross:
             self.cross.start()
         if self.core:
             self.pass_on[plane][0].start()
@@ -110,28 +112,30 @@
     V = pltpu.VMEM
     D = pltpu.SemaphoreType.DMA
     return dict(
-        kv=V((2, 4, 2, 2, 768, 128), BF),
-        kx=V((2, 4, 2, 768, 256), BF),
-        vt=V((2, 4, 2, 144, 768), BF),
+        kv=V((12, 2, 2, 768, 128), BF),
+        kx=V((12, 2, 768, 256), BF),
+        vt=V((12, 2, 144, 768), BF),
+        score0=V((768, 512), F32),
+        score1=V((768, 512), F32),
+        top0=V((8, 512), F32),
+        top1=V((8, 512), F32),
         qa=V((3, 2, 512, 256), BF),
-        tq_in=V((128, 1024), BF),
         sq_in=V((128, 512), BF),
         m=V((3, 2, 8, 512), F32),
         acc=V((3, 2, 144, 512), F32),
-        o_out=V((3, 2, 128, 512), BF),
-        o_in=V((3, 2, 128, 512), BF),
-        l_out=V((3, 2, 8, 512), F32),
-        l_in=V((3, 2, 8, 512), F32),
+        o_out=V((2, 128, 512), BF),
+        o_in=V((2, 128, 512), BF),
+        l_out=V((2, 8, 512), F32),
+        l_in=V((2, 8, 512), F32),
         tctx=V((8, 2, 128, 1024), BF),
         sctx=V((8, 2, 128, 512), BF),
         tw=V((1024, 512), BF),
         sw=V((512, 256), BF),
-        mp=V((8, 512, 512), BF),
         ty_out=V((2, 128, 512), BF),
         ty_in=V((2, 128, 512), BF),
         sy_out=V((256, 256), BF),
         sy_in=V((256, 256), BF),
-        tpart=V((2, 4, 2, 128, 512), F32),
+        tpart=V((4, 2, 128, 512), F32),
         spart=V((4, 2, 256, 256), F32),
         tr_out=V((2, 2, 128, 512), BF),
         tr_in=V((2, 2, 2, 64, 512), BF),
@@ -172,32 +176,35 @@
     right, left, across, core = seq_dev(0, 1, 0), seq_dev(0, 3, 0), seq_dev(1, 0, 0), seq_dev(0, 0, 1)
 
     loads = [
-        pltpu.make_async_copy(skv_h, b["kv"].at[0, x, c], b["loc"].at[0]),
-        pltpu.make_async_copy(tkv_h, b["kv"].at[1, x, c], b["loc"].at[1]),
+        pltpu.make_async_copy(skv_h, b["kv"].at[x, c], b["loc"].at[0]),
+        pltpu.make_async_copy(tkv_h, b["kv"].at[4 + k_own, c], b["loc"].at[1]),
         pltpu.make_async_copy(sw_h, b["sw"], b["loc"].at[2]),
         pltpu.make_async_copy(tw_h, b["tw"], b["loc"].at[3]),
-        pltpu.make_async_copy(mp_h, b["mp"], b["loc"].at[4]),
     ]
     for load in loads:
         load.start()
+    map_loads = [
+        pltpu.make_async_copy(
+            mp_h.at[:, :, pl.ds(u * 256, 256)], b["kx"].at[pl.ds(0, 8), u, pl.ds(0, 512)], b["loc"].at[4 + u]
+        )
+        for u in range(2)
+    ]
 
     barrier = pltpu.get_barrier_semaphore()
     for off in range(1, 16):
         pl.semaphore_signal(barrier, inc=1, device_id=((s + off) % 16, p), device_id_type=MESH)
     for off in range(1, 8):
         pl.semaphore_signal(barrier, inc=1, device_id=(s, (p + off) % 8), device_id_type=MESH)
-    pl.semaphore_wait(barrier, 22)
 
     wire = Wire(b["wsend"], b["wrecv"])
     give_sq = wire.copy(sq, b["sq_in"], across)
-    give_tq = wire.copy(tq, b["tq_in"], across)
 
     def kv_block(model):
         def block(plane, off, part):
-            at = (x + off) % 4
+            at = (x + off) % 4 + model * (4 + ((yh + plane) % 2) * 4)
             if part is None:
-                return b["kv"].at[model, at, c]
-            return b["kv"].at[model, at, c, part]
+                return b["kv"].at[at, c]
+            return b["kv"].at[at, c, part]
 
         return block
 
@@ -232,13 +239,15 @@
         return block
 
     g_skv = Gather(wire, kv_block(0), right, left, None, core)
-    g_tkv = Gather(wire, kv_block(1), right, left, None, core)
+    g_tkv = Gather(wire, kv_block(1), right, left, across, core)
+    keys_sent = len(wire.made)
     g_s = Gather(wire, s_block, right, left, None, core, 2)
-    g_t = [Gather(wire, t_block(half), right, left, None, core, 2) for half in range(2)]
+    g_t = [Gather(wire, t_block(half), right, left, across, core) for half in range(2)]
+    contexts_sent = len(wire.made)
     g_n = Gather(wire, nb_block, right, left, across, core)
     g_d = [Gather(wire, dl_block(half), tp_dev(0, 1), tp_dev(0, 3), tp_dev(1, 0), None) for half in range(2)]
-    give_o = [[wire.copy(b["o_out"].at[i, 1 - g], b["o_in"].at[i, g], across) for g in range(2)] for i in range(3)]
-    give_l = [[wire.copy(b["l_out"].at[i, 1 - g], b["l_in"].at[i, g], across) for g in range(2)] for i in range(3)]
+    give_o = [wire.copy(b["o_out"].at[1 - g], b["o_in"].at[g], across) for g in range(2)]
+    give_l = [wire.copy(b["l_out"].at[1 - g], b["l_in"].at[g], across) for g in range(2)]
     s_sq = [wire.copy(b["ssq"].at[s], b["ssq"].at[s], ((s + off) % 16, p)) for off in range(1, 16)]
     t_sq = [
         [wire.copy(b["tsq"].at[half, s], b["tsq"].at[half, s], ((s + off) % 16, p)) for off in range(1, 16)]
@@ -260,90 +269,133 @@
             rows = slice(h * tokens[one], (h + 1) * tokens[one])
             qa[one, group, rows, 0:128] = src[first : first + tokens[one], h * 128 : (h + 1) * 128]
 
-    def prepare(model, passes):
+    def prepare(first, last, passes):
         rows = lax.broadcasted_iota(jnp.int32, (128, 128), 0)
         lanes = lax.broadcasted_iota(jnp.int32, (128, 128), 1)
         for one in passes:
             eye = jnp.where(rows % tokens[one] + 64 * (one // 2) == lanes, 1.0, 0.0).astype(BF)
-            for g in range(2):
+            for g in range(2 if one == 0 else 1):
                 for i in range(4):
                     qa[one, g, i * 128 : (i + 1) * 128, 128:256] = eye
             m[one] = jnp.full((2, 8, 512), HIDDEN, F32)
             acc[one] = jnp.zeros((2, 144, 512), F32)
 
         def extra(i, carry):
-            b["kx"][model, i, :, :, 128:256] = jnp.zeros((2, 768, 128), BF)
-            b["vt"][model, i, :, 128:144, :] = jnp.ones((2, 16, 768), BF)
+            b["kx"][i, :, :, 128:256] = jnp.zeros((2, 768, 128), BF)
+            b["vt"][i, :, 128:144, :] = jnp.ones((2, 16, 768), BF)
             return carry
 
-        lax.fori_loop(0, 4, extra, 0)
+        lax.fori_loop(first, last, extra, 0)
 
     first_key = doc[0]
 
+    def tile_at(n, u):
+        third = n // 8
+        t = (third + 1) // 2
+        other = third // 2
+        one = t * (1 + (1 - other) * ((n % 8) // 4) + other * (n % 2))
+        i = (1 - t + other) * ((n % 8) // 2) + (t - other) * (n % 4)
+        plane = (yh + other) % 2
+        at = (x + 3 * i + 3 * (i // 2) + 2 * (i // 3)) % 4
+        from_core = (c + (1 - t) * (n % 2) + t * u) % 2
+        return one, (1 - t) * u, t * (4 + plane * 4) + at, plane, at, from_core
+
+    def build(n, u):
+        one, g, block, plane, at, from_core = tile_at(n, u)
+        base = (plane * 4 + at) * KEYS_CHIP + from_core * 768
+
+        @pl.when((one <= 1) if u == 0 else (one == 1))
+        def _():
+            b["vt"][block, from_core, 0:128, :] = b["kv"][block, from_core, 1].T
+            b["kx"][block, from_core, :, 0:128] = b["kv"][block, from_core, 0]
+
+            @pl.when(plane == 0)
+            def _():
+                key = lax.broadcasted_iota(jnp.int32, (768, 128), 0)
+                b["kx"][block, from_core, :, 128:256] = jnp.where(key >= first_key - base, 0.0, HIDDEN).astype(BF)
+
+        @pl.when((one <= 1) & (plane == 1) & (at >= 2))
+        def _():
+            ahead = CACHE + ((((yh + g) % 2) * 4 + x) * 2 + c) * 128 - base
+            key = lax.broadcasted_iota(jnp.int32, (768, 128), 0)
+            row = lax.broadcasted_iota(jnp.int32, (768, 128), 1)
+            b["kx"][block, from_core, :, 128:256] = jnp.where(key - row <= ahead, 0.0, HIDDEN).astype(BF)
+
+    scores, tops = (b["score0"], b["score1"]), (b["top0"], b["top1"])
+
+    def overlapped(n, u, weigh_n, weigh=True):
+        one, g, block, _, _, from_core = tile_at(n, u)
+        queries = qa[one, g]
+        top = jnp.full((8, 512), HIDDEN, F32)
+        if weigh:
+            w_one, w_g, w_block, _, _, w_core = tile_at(weigh_n, 1 - u)
+            old = m[w_one, w_g]
+            peak = jnp.max(tops[1 - u][...], axis=0, keepdims=True)
+            new = jnp.maximum(old, jnp.broadcast_to(peak, (8, 512)))
+            total = (acc[w_one, w_g].reshape(18, 8, 512) * jnp.exp2((old - new) * SCALE)[None]).reshape(144, 512)
+        for j in range(3):
+            keys = slice(j * 256, (j + 1) * 256)
+            fresh = dot(b["kx"][block, from_core, keys, :], queries, ((1,), (1,)))
+            scores[u][keys, :] = fresh
+            top = jnp.maximum(top, jnp.max(fresh.reshape(32, 8, 512), axis=0))
+            if weigh:
+                held = scores[1 - u][keys, :].reshape(32, 8, 512)
+                weights = jnp.exp2((held - new[None]) * SCALE).reshape(256, 512).astype(BF)
+                total = total + dot(b["vt"][w_block, w_core, :, keys], weights)
+        tops[u][...] = top
+        if weigh:
+            m[w_one, w_g] = new
+            acc[w_one, w_g] = total
+
     def attention(hooks):
+        build(0, 0)
+        overlapped(0, 0, 0, weigh=False)
+
         def step(n, carry):
             for at_step, hook in hooks.items():
                 pl.when(n == at_step)(hook)
-            one, i, half, g = n // 16, (n % 16) // 4, (n % 4) // 2, n % 2
-            model = (one + 1) // 2
-            at = (x + 3 * i + 3 * (i // 2) + 2 * (i // 3)) % 4
-            from_core = (c + half) % 2
-            base = (yh * 4 + at) * KEYS_CHIP + from_core * 768
-
-            @pl.when((g == 0) & (one <= 1))
-            def _():
-                b["vt"][model, at, from_core, 0:128, :] = b["kv"][model, at, from_core, 1].T
-                b["kx"][model, at, from_core, :, 0:128] = b["kv"][model, at, from_core, 0]
-
-            @pl.when((yh == 0) & (g == 0) & (one <= 1))
-            def _():
-                key = lax.broadcasted_iota(jnp.int32, (768, 128), 0)
-                b["kx"][model, at, from_core, :, 128:256] = jnp.where(key >= first_key - base, 0.0, HIDDEN).astype(BF)
-
-            @pl.when((yh == 1) & (at >= 2))
-            def _():
-                first_row = CACHE + ((((yh + g) % 2) * 4 + x) * 2 + c) * 128
-                key = lax.broadcasted_iota(jnp.int32, (768, 128), 0)
-                row = lax.broadcasted_iota(jnp.int32, (768, 128), 1)
-                b["kx"][model, at, from_core, :, 128:256] = jnp.where(key - row <= first_row - base, 0.0, HIDDEN).astype(BF)
-
-            scores = dot(b["kx"][model, at, from_core], qa[one, g], ((1,), (1,)))
-            old = m[one, g]
-            new = jnp.maximum(old, jnp.broadcast_to(jnp.max(scores, axis=0, keepdims=True), (8, 512)))
-            weights = jnp.exp2((scores.reshape(96, 8, 512) - new[None]) * SCALE).reshape(768, 512).astype(BF)
-            shrink = jnp.exp2((old - new) * SCALE)
-            fresh = dot(b["vt"][model, at, from_core], weights)
-            m[one, g] = new
-            acc[one, g] = (acc[one, g].reshape(18, 8, 512) * shrink[None]).reshape(144, 512) + fresh
+            build(n, 1)
+            overlapped(n, 1, n)
+            after = (n + 1) % 24
+            build(after, 0)
+            overlapped(after, 0, n)
             return carry
 
-        lax.fori_loop(0, 48, step, 0)
+        lax.fori_loop(0, 24, step, 0)
 
     def part_of(one, g):
         total = acc[one, g, 128:136, :]
         mean = (acc[one, g, 0:128, :].reshape(16, 8, 512) * (1.0 / total)[None]).reshape(128, 512)
         return mean, m[one, g] * SCALE + jnp.log(total) * LOG2E
 
-    def partner_part(one):
+    def partner_part():
         for g in (1, 0):
-            mean, logs = part_of(one, g)
-            b["o_out"][one, g] = mean.astype(BF)
-            b["l_out"][one, g] = logs
-            give_o[one][1 - g].start()
-            give_l[one][1 - g].start()
-
-    def combine(one, g, ctx):
-        give_o[one][g].wait_recv()
-        give_l[one][g].wait_recv()
-        mine, log_mine = part_of(one, g)
-        share = 1.0 / (1.0 + jnp.exp2(log_mine - b["l_in"][one, g]))
-        other = b["o_in"][one, g].astype(F32)
-        both = mine + ((other - mine).reshape(16, 8, 512) * share[None]).reshape(128, 512)
+            mean, logs = part_of(0, g)
+            b["o_out"][g] = mean.astype(BF)
+            b["l_out"][g] = logs
+            give_o[1 - g].start()
+            give_l[1 - g].start()
+
+    def keep_context(one, plane, both, ctx):
         both = both.T.astype(BF)
         count, first = tokens[one], 64 * (one // 2)
         for h in range(heads[one]):
             held = both[h * count : (h + 1) * count, :]
-            ctx[((yh + g) % 2) * 4 + x, c, first : first + count, h * 128 : (h + 1) * 128] = held
+            ctx[plane * 4 + x, c, first : first + count, h * 128 : (h + 1) * 128] = held
+
+    def s_context(g):
+        give_o[g].wait_recv()
+        give_l[g].wait_recv()
+        mine, log_mine = part_of(0, g)
+        share = 1.0 / (1.0 + jnp.exp2(log_mine - b["l_in"][g]))
+        other = b["o_in"][g].astype(F32)
+        both = mine + ((other - mine).reshape(16, 8, 512) * share[None]).reshape(128, 512)
+        keep_context(0, (yh + g) % 2, both, b["sctx"])
+        g_s.root(g)
+
+    def t_context(half):
+        keep_context(1 + half, yh, part_of(1 + half, 0)[0], b["tctx"])
+        g_t[half].root(0)
 
     class Reduce:
         def __init__(self, ctx, w, name, half):
@@ -352,7 +404,7 @@
             def of(key):
                 return b[name + key] if half is None else b[name + key].at[half]
 
-            self.y_out, self.y_in, self.part, self.hid = of("y_out"), of("y_in"), of("part"), of("hid")
+            self.y_out, self.y_in, self.part, self.hid = of("y_out"), of("y_in"), b[name + "part"], of("hid")
             self.r_out, self.r_in, self.z_out, self.z_in = of("r_out"), of("r_in"), of("z_out"), of("z_in")
             self.rows = self.part.shape[2] // 2
             near = (tp_dev(0, 3), tp_dev(0, 1))
@@ -441,38 +493,32 @@
         gather.have_near(plane)
         gather.have_far(plane)
 
+    fill_queries(0, sq, 0)
+    prepare(0, 4, (0,))
+    loads[0].wait()
+    loads[1].wait()
+    pl.semaphore_wait(barrier, 22)
+    g_skv.root(0)
     give_sq.start()
-    loads[0].wait()
-    g_skv.root(0)
-    give_tq.start()
-    fill_queries(0, sq, 0)
-    prepare(0, (0,))
+    g_tkv.cross.start()
 
     def s_partner():
+        g_skv.have_own(0)
         give_sq.wait_recv()
         fill_queries(0, b["sq_in"], 1)
 
     def s_near():
-        prepare(1, (1, 2))
+        prepare(4, 12, (1, 2))
         fill_queries(1, tq, 0)
         fill_queries(2, tq, 0)
-        loads[1].wait()
         g_skv.mid(0)
-        g_tkv.root(0)
+        g_tkv.root(0, False)
 
     def t_start():
-        partner_part(0)
-        give_tq.wait_recv()
-        fill_queries(1, b["tq_in"], 1)
-        fill_queries(2, b["tq_in"], 1)
-
-    def t_near():
+        partner_part()
+        g_tkv.have_own(0)
         g_tkv.mid(0)
-        g_tkv.have_own(0)
-
-    def context(one, g, ctx, gather):
-        combine(one, g, ctx)
-        gather.root(g)
+        g_tkv.root(1)
 
     def s_sums():
         for load in loads[2:]:
@@ -494,72 +540,79 @@
     def t1_sums():
         r_t[0].multiply(0, 4, {0: lambda: ready(g_t[0], 0), 2: lambda: ready(g_t[0], 1)})
 
-    def s_last_spread():
-        g_s.mid(1)
-        g_s.far(0)
-
-    def s_squares_t1():
-        s_squares()
-        g_t[0].mid(0)
-
-    def t1_spread():
-        g_t[0].mid(1)
-        g_t[0].far(0)
-
-    def last():
-        g_n.mid(0)
-        t1_sums()
+    def both(*hooks):
+        def run():
+            for hook in hooks:
+                hook()
+
+        return run
 
     attention(
         {
-            1: s_partner,
-            2: lambda: g_skv.have_own(0),
-            4: s_near,
-            6: lambda: g_skv.have_left(0),
-            10: lambda: g_skv.have_right(0),
-            12: lambda: g_skv.far(0),
-            14: lambda: g_skv.have_far(0),
-            16: t_start,
-            18: t_near,
-            21: lambda: context(0, 0, b["sctx"], g_s),
-            22: lambda: g_tkv.have_left(0),
-            25: lambda: context(0, 1, b["sctx"], g_s),
-            26: lambda: g_tkv.have_right(0),
-            27: lambda: g_s.mid(0),
-            28: lambda: g_tkv.far(0),
-            29: s_last_spread,
-            30: lambda: g_tkv.have_far(0),
-            31: lambda: g_s.far(1),
-            32: lambda: partner_part(1),
-            33: s_sums,
-            35: r_s.send_on,
-            37: lambda: context(1, 0, b["tctx"], g_t[0]),
-            39: r_s.settle,
-            41: lambda: context(1, 1, b["tctx"], g_t[0]),
-            42: s_squares_t1,
-            44: s_normed,
-            45: t1_spread,
-            46: lambda: g_t[0].far(1),
-            47: last,
+            0: s_partner,
+            1: s_near,
+            2: lambda: g_skv.have_left(0),
+            4: lambda: g_skv.have_right(0),
+            5: lambda: g_skv.far(0),
+            6: lambda: g_skv.have_far(0),
+            8: t_start,
+            9: lambda: g_tkv.have_left(0),
+            10: both(lambda: g_tkv.have_right(0), lambda: g_tkv.far(0)),
+            11: lambda: g_tkv.have_far(0),
+            12: lambda: s_context(0),
+            16: both(lambda: g_tkv.have_own(1), lambda: s_context(1)),
+            17: lambda: g_tkv.mid(1),
+            18: both(lambda: g_tkv.have_left(1), lambda: g_s.mid(0)),
+            20: both(lambda: g_tkv.have_right(1), lambda: g_s.mid(1), lambda: g_s.far(0)),
+            21: lambda: g_tkv.far(1),
+            22: both(lambda: g_tkv.have_far(1), lambda: g_s.far(1)),
+            23: lambda: t_context(0),
         }
     )
-    partner_part(2)
+    for load in map_loads:
+        load.start()
+    t_context(1)
+    s_sums()
+    g_t[0].mid(0)
+    g_t[0].root(1)
+    r_s.send_on()
+    g_t[1].mid(0)
+    g_t[1].root(1)
+    g_t[0].far(0)
+    g_t[0].mid(1)
+    r_s.settle()
+    wire.close(0, keys_sent)
+    g_t[0].far(1)
+    t1_sums()
+    s_squares()
+    g_t[1].far(0)
+    g_t[1].mid(1)
+    r_t[0].send_on()
+    s_normed()
+    g_t[1].far(1)
+    r_t[0].settle()
+    g_n.mid(0)
     g_n.root(1)
-    r_t[0].send_on()
+    r_t[1].multiply(0, 4, {0: lambda: ready(g_t[1], 0), 2: lambda: ready(g_t[1], 1)})
+    r_t[0].finish(tres)
+    send_squares(b["thid"].at[0], b["tsq"].at[0], t_sq[0])
     g_n.far(0)
     g_n.mid(1)
-    context(2, 0, b["tctx"], g_t[1])
+    r_t[1].send_on()
+    wire.close(keys_sent, contexts_sent)
     g_n.far(1)
-    r_t[0].settle()
     for made in n_tp:
         made.start()
     ready(g_n, 0)
     ready(g_n, 1)
     b["diff"][...] = jnp.zeros((2, 128, 512), F32)
+    for load in map_loads:
+        load.wait()
 
     def match(k, carry):
         lhs = jnp.concatenate([b["nb"][2 * k], b["nb"][2 * k + 1]], axis=1)
-        b["diff"][...] += dot(lhs, b["mp"][k]).reshape(2, 128, 512)
+        for u in range(2):
+            b["diff"][:, :, u * 256 : (u + 1) * 256] += dot(lhs, b["kx"][k, u, 0:512, :]).reshape(2, 128, 256)
         return carry
 
     lax.fori_loop(0, 8, match, 0)
@@ -583,43 +636,33 @@
         lax.fori_loop(0, offs[2], one, 0)
 
     own, near, far = (0, 1, 1), (1, 2, 2), (2, 1, 1)
-    context(2, 1, b["tctx"], g_t[1])
-    g_t[1].mid(0)
-    g_t[1].far(0)
-    r_t[0].finish(tres)
-    send_squares(b["thid"].at[0], b["tsq"].at[0], t_sq[0])
-    r_t[1].multiply(0, 2, {0: lambda: ready(g_t[1], 0)})
-    g_t[1].mid(1)
-    g_t[1].far(1)
+    r_t[1].settle()
     delta(0)
-    r_t[1].multiply(2, 4, {2: lambda: ready(g_t[1], 1)})
+    r_t[1].finish(tres)
+    send_squares(b["thid"].at[1], b["tsq"].at[1], t_sq[1])
+    b["ng"][p, 0] = b["nb"][2 * p]
+    b["ng"][p, 1] = b["nb"][2 * p + 1]
+    out[...] = jnp.zeros((512, 512), F32)
+    g_d[0].mid(0)
+    g_d[0].root(1)
+    delta(1)
     for made, onward in zip(n_tp, n_core):
         made.wait_recv()
         onward.start()
-    b["ng"][p, 0] = b["nb"][2 * p]
-    b["ng"][p, 1] = b["nb"][2 * p + 1]
-    out[...] = jnp.zeros((512, 512), F32)
-    r_t[1].send_on()
-    g_d[0].mid(0)
-    g_d[0].root(1)
+    g_d[0].far(0)
+    g_d[0].mid(1)
     for made in n_core:
         made.wait_recv()
     gradient(0, 0, own)
     gradient(0, 0, near)
-    r_t[1].settle()
-    g_d[0].far(0)
-    g_d[0].mid(1)
-    r_t[1].finish(tres)
-    send_squares(b["thid"].at[1], b["tsq"].at[1], t_sq[1])
     gradient(0, 0, far)
     gradient(0, 1, own)
-    delta(1)
+    g_d[1].mid(0)
+    g_d[1].root(1)
     gradient(0, 1, near)
     g_d[0].far(1)
     gradient(0, 1, far)
     gradient(1, 0, own)
-    g_d[1].mid(0)
-    g_d[1].root(1)
     gradient(1, 0, near)
     gradient(1, 1, own)
     g_d[1].far(0)

time: 168 us -> 154 us (0.917)
  Pallas kernels: 165 us -> 151 us
    pallas_call x1, Pallas kernels: 165 us -> 151 us  [per_device(): pl.pallas_call(kernel, out_shape=jax.ShapeDtypeStruct((512, 512), F32), i...]
where the time goes in v2:
time: 154 us
  Pallas kernels  151 us (98%)
  local copies, waits for them, and re-layouts  2.26 us (1%)
    pallas_call x1, Pallas kernels, per_device(): pl.pallas_call(kernel, out_shape=jax.ShapeDtypeStruct((512, 512), F32), i...  151 us

profile of v2, /device:TPU:0, one launch (start us, length us, event | category | flops | bytes accessed | tf_op | source)
XLA Modules:
  0.0 153.8 jit_solution(12721905970965937921)
XLA Ops:
  0.7 150.9 %shard_map.118 = f32[512,512]{1,0:T(8,128)} custom-call(s32[1]{0:T(128)S(6)} %copy.14.doc, bf16[128,1024]{1,0:T(8,128)(2,1)} %tq.1, bf16[2,768,128]{2,1,0:T(8,128)(2,1)} %tkv_h.1, bf16[128,512]{1,0:T(8,128)(2,1)} %sq.1, bf16[2,768,128]{2,1,0:T(8,128)(2,1)} %skv_h.1, bf16[256,512]{1,0:T(8,128)(2,1)} %tres.1, bf16[1024,512]{1,0:T(8,128)(2,1)} %tw_h.1, ...), custom_call_target="tpu_custom_call" | custom-call | tf_op jit(solution)/shard_map/pallas_call | solution.py:681
  151.6 2.3 %copy.15 = f32[512,512]{1,0:T(8,128)} copy(f32[512,512]{1,0:T(8,128)} %shard_map.118) | data formatting | bytes 2097152

commit v3 on v2

--- a/solution.py
+++ b/solution.py
@@ -153,8 +153,8 @@
         ng=V((8, 2, 256, 256), BF),
         dl=V((2, 8, 128, 512), BF),
         diff=V((2, 128, 512), F32),
-        wsend=D((200,)),
-        wrecv=D((200,)),
+        wsend=D((208,)),
+        wrecv=D((208,)),
         loc=D((8,)),
     )
 
@@ -253,8 +253,19 @@
         [wire.copy(b["tsq"].at[half, s], b["tsq"].at[half, s], ((s + off) % 16, p)) for off in range(1, 16)]
         for half in range(2)
     ]
+    half_rows = pl.ds((x % 2) * 128, 128)
+    beside_x = seq_dev(0, 1 + 2 * (x % 2), 0)
     n_tp = [
-        wire.copy(b["nb"].at[((p + off) % 8) * 2 + c], b["ng"].at[p, c], (s, (p + off) % 8)) for off in range(1, 8)
+        wire.copy(
+            b["nb"].at[((p + off) % 8) * 2 + c, half_rows], b["ng"].at[p, c, half_rows], (s, (p + off) % 8)
+        )
+        for off in range(1, 8)
+    ]
+    n_x = [
+        wire.copy(
+            b["ng"].at[(p + 8 - off) % 8, c, half_rows], b["ng"].at[(p + 8 - off) % 8, c, half_rows], beside_x
+        )
+        for off in range(1, 8)
     ]
     n_core = [
         wire.copy(b["ng"].at[(p + 8 - off) % 8, c], b["ng"].at[(p + 8 - off) % 8, c], core) for off in range(1, 8)
@@ -566,16 +577,15 @@
             20: both(lambda: g_tkv.have_right(1), lambda: g_s.mid(1), lambda: g_s.far(0)),
             21: lambda: g_tkv.far(1),
             22: both(lambda: g_tkv.have_far(1), lambda: g_s.far(1)),
-            23: lambda: t_context(0),
+            23: both(lambda: t_context(0), s_sums),
         }
     )
     for load in map_loads:
         load.start()
     t_context(1)
-    s_sums()
+    r_s.send_on()
     g_t[0].mid(0)
     g_t[0].root(1)
-    r_s.send_on()
     g_t[1].mid(0)
     g_t[1].root(1)
     g_t[0].far(0)
@@ -646,7 +656,10 @@
     g_d[0].mid(0)
     g_d[0].root(1)
     delta(1)
-    for made, onward in zip(n_tp, n_core):
+    for made, onward in zip(n_tp, n_x):
+        made.wait_recv()
+        onward.start()
+    for made, onward in zip(n_x, n_core):
         made.wait_recv()
         onward.start()
     g_d[0].far(0)

time: 154 us -> 161 us (1.045)
  Pallas kernels: 151 us -> 157 us
    pallas_call x1, Pallas kernels: 151 us -> 157 us  [per_device(): pl.pallas_call(kernel, out_shape=jax.ShapeDtypeStruct((512, 512), F32), i...]
where the time goes in v3:
time: 161 us; the launch traced here: 160 us
  Pallas kernels  157 us (98%)
  local copies, waits for them, and re-layouts  2.26 us (1%)
    pallas_call x1, Pallas kernels, per_device(): pl.pallas_call(kernel, out_shape=jax.ShapeDtypeStruct((512, 512), F32), i...  157 us

profile of v3, /device:TPU:0, one launch (start us, length us, event | category | flops | bytes accessed | tf_op | source)
XLA Modules:
  0.0 160.1 jit_solution(5495502466326515896)
XLA Ops:
  0.7 157.2 %shard_map.118 = f32[512,512]{1,0:T(8,128)} custom-call(s32[1]{0:T(128)S(6)} %copy.14.doc, bf16[128,1024]{1,0:T(8,128)(2,1)} %tq.1, bf16[2,768,128]{2,1,0:T(8,128)(2,1)} %tkv_h.1, bf16[128,512]{1,0:T(8,128)(2,1)} %sq.1, bf16[2,768,128]{2,1,0:T(8,128)(2,1)} %skv_h.1, bf16[256,512]{1,0:T(8,128)(2,1)} %tres.1, bf16[1024,512]{1,0:T(8,128)(2,1)} %tw_h.1, ...), custom_call_target="tpu_custom_call" | custom-call | tf_op jit(solution)/shard_map/pallas_call | solution.py:694
  157.9 2.3 %copy.15 = f32[512,512]{1,0:T(8,128)} copy(f32[512,512]{1,0:T(8,128)} %shard_map.118) | data formatting | bytes 2097152

commit v4 on v2

--- a/solution.py
+++ b/solution.py
@@ -135,7 +135,7 @@
         ty_in=V((2, 128, 512), BF),
         sy_out=V((256, 256), BF),
         sy_in=V((256, 256), BF),
-        tpart=V((4, 2, 128, 512), F32),
+        tpart=V((2, 4, 2, 128, 512), F32),
         spart=V((4, 2, 256, 256), F32),
         tr_out=V((2, 2, 128, 512), BF),
         tr_in=V((2, 2, 2, 64, 512), BF),
@@ -404,7 +404,7 @@
             def of(key):
                 return b[name + key] if half is None else b[name + key].at[half]
 
-            self.y_out, self.y_in, self.part, self.hid = of("y_out"), of("y_in"), b[name + "part"], of("hid")
+            self.y_out, self.y_in, self.part, self.hid = of("y_out"), of("y_in"), of("part"), of("hid")
             self.r_out, self.r_in, self.z_out, self.z_in = of("r_out"), of("r_in"), of("z_out"), of("z_in")
             self.rows = self.part.shape[2] // 2
             near = (tp_dev(0, 3), tp_dev(0, 1))
@@ -560,49 +560,53 @@
             10: both(lambda: g_tkv.have_right(0), lambda: g_tkv.far(0)),
             11: lambda: g_tkv.have_far(0),
             12: lambda: s_context(0),
-            16: both(lambda: g_tkv.have_own(1), lambda: s_context(1)),
-            17: lambda: g_tkv.mid(1),
-            18: both(lambda: g_tkv.have_left(1), lambda: g_s.mid(0)),
-            20: both(lambda: g_tkv.have_right(1), lambda: g_s.mid(1), lambda: g_s.far(0)),
-            21: lambda: g_tkv.far(1),
-            22: both(lambda: g_tkv.have_far(1), lambda: g_s.far(1)),
+            15: lambda: s_context(1),
+            16: lambda: g_tkv.have_own(1),
+            17: both(lambda: g_tkv.mid(1), lambda: g_s.mid(0)),
+            18: lambda: g_tkv.have_left(1),
+            19: both(lambda: g_s.mid(1), lambda: g_s.far(0)),
+            20: lambda: g_tkv.have_right(1),
+            21: both(lambda: g_tkv.far(1), lambda: g_s.far(1)),
+            22: both(lambda: g_tkv.have_far(1), s_sums),
             23: lambda: t_context(0),
         }
     )
     for load in map_loads:
         load.start()
     t_context(1)
-    s_sums()
+    r_s.send_on()
     g_t[0].mid(0)
     g_t[0].root(1)
-    r_s.send_on()
     g_t[1].mid(0)
     g_t[1].root(1)
+    wire.close(0, keys_sent)
     g_t[0].far(0)
     g_t[0].mid(1)
     r_s.settle()
-    wire.close(0, keys_sent)
     g_t[0].far(1)
     t1_sums()
-    s_squares()
     g_t[1].far(0)
     g_t[1].mid(1)
+    s_squares()
+    g_t[1].far(1)
     r_t[0].send_on()
+    r_t[1].multiply(0, 4, {0: lambda: ready(g_t[1], 0), 2: lambda: ready(g_t[1], 1)})
     s_normed()
-    g_t[1].far(1)
+    r_t[1].send_on()
     r_t[0].settle()
     g_n.mid(0)
     g_n.root(1)
-    r_t[1].multiply(0, 4, {0: lambda: ready(g_t[1], 0), 2: lambda: ready(g_t[1], 1)})
     r_t[0].finish(tres)
     send_squares(b["thid"].at[0], b["tsq"].at[0], t_sq[0])
     g_n.far(0)
     g_n.mid(1)
-    r_t[1].send_on()
-    wire.close(keys_sent, contexts_sent)
+    r_t[1].settle()
     g_n.far(1)
     for made in n_tp:
         made.start()
+    r_t[1].finish(tres)
+    send_squares(b["thid"].at[1], b["tsq"].at[1], t_sq[1])
+    wire.close(keys_sent, contexts_sent)
     ready(g_n, 0)
     ready(g_n, 1)
     b["diff"][...] = jnp.zeros((2, 128, 512), F32)
@@ -636,16 +640,13 @@
         lax.fori_loop(0, offs[2], one, 0)
 
     own, near, far = (0, 1, 1), (1, 2, 2), (2, 1, 1)
-    r_t[1].settle()
     delta(0)
-    r_t[1].finish(tres)
-    send_squares(b["thid"].at[1], b["tsq"].at[1], t_sq[1])
+    delta(1)
     b["ng"][p, 0] = b["nb"][2 * p]
     b["ng"][p, 1] = b["nb"][2 * p + 1]
     out[...] = jnp.zeros((512, 512), F32)
     g_d[0].mid(0)
     g_d[0].root(1)
-    delta(1)
     for made, onward in zip(n_tp, n_core):
         made.wait_recv()
         onward.start()

time: 154 us -> 157 us (1.019)
  Pallas kernels: 151 us -> 154 us
    pallas_call x1, Pallas kernels: 151 us -> 154 us  [per_device(): pl.pallas_call(kernel, out_shape=jax.ShapeDtypeStruct((512, 512), F32), i...]
where the time goes in v4:
time: 157 us
  Pallas kernels  154 us (98%)
  local copies, waits for them, and re-layouts  2.26 us (1%)
    pallas_call x1, Pallas kernels, per_device(): pl.pallas_call(kernel, out_shape=jax.ShapeDtypeStruct((512, 512), F32), i...  154 us

profile of v4, /device:TPU:0, one launch (start us, length us, event | category | flops | bytes accessed | tf_op | source)
XLA Modules:
  0.0 156.7 jit_solution(9804676854782272942)
XLA Ops:
  0.7 153.7 %shard_map.118 = f32[512,512]{1,0:T(8,128)} custom-call(s32[1]{0:T(128)S(6)} %copy.14.doc, bf16[128,1024]{1,0:T(8,128)(2,1)} %tq.1, bf16[2,768,128]{2,1,0:T(8,128)(2,1)} %tkv_h.1, bf16[128,512]{1,0:T(8,128)(2,1)} %sq.1, bf16[2,768,128]{2,1,0:T(8,128)(2,1)} %skv_h.1, bf16[256,512]{1,0:T(8,128)(2,1)} %tres.1, bf16[1024,512]{1,0:T(8,128)(2,1)} %tw_h.1, ...), custom_call_target="tpu_custom_call" | custom-call | tf_op jit(solution)/shard_map/pallas_call | solution.py:682
  154.4 2.3 %copy.15 = f32[512,512]{1,0:T(8,128)} copy(f32[512,512]{1,0:T(8,128)} %shard_map.118) | data formatting | bytes 2097152

commit v5 on v4

--- a/solution.py
+++ b/solution.py
@@ -119,7 +119,7 @@
         score1=V((768, 512), F32),
         top0=V((8, 512), F32),
         top1=V((8, 512), F32),
-        qa=V((3, 2, 512, 256), BF),
+        qa=V((3, 2, 256, 512), BF),
         sq_in=V((128, 512), BF),
         m=V((3, 2, 8, 512), F32),
         acc=V((3, 2, 144, 512), F32),
@@ -265,18 +265,22 @@
 
     def fill_queries(one, src, group):
         first = 64 * (one // 2)
-        for h in range(heads[one]):
-            rows = slice(h * tokens[one], (h + 1) * tokens[one])
-            qa[one, group, rows, 0:128] = src[first : first + tokens[one], h * 128 : (h + 1) * 128]
+        for i in range(4):
+            if one == 0:
+                held = src[:, i * 128 : (i + 1) * 128]
+            else:
+                pair = [src[first : first + 64, h * 128 : (h + 1) * 128] for h in (2 * i, 2 * i + 1)]
+                held = jnp.concatenate(pair, axis=0)
+            qa[one, group, 0:128, i * 128 : (i + 1) * 128] = held.T
 
     def prepare(first, last, passes):
         rows = lax.broadcasted_iota(jnp.int32, (128, 128), 0)
         lanes = lax.broadcasted_iota(jnp.int32, (128, 128), 1)
         for one in passes:
-            eye = jnp.where(rows % tokens[one] + 64 * (one // 2) == lanes, 1.0, 0.0).astype(BF)
+            eye = jnp.where(lanes % tokens[one] + 64 * (one // 2) == rows, 1.0, 0.0).astype(BF)
             for g in range(2 if one == 0 else 1):
                 for i in range(4):
-                    qa[one, g, i * 128 : (i + 1) * 128, 128:256] = eye
+                    qa[one, g, 128:256, i * 128 : (i + 1) * 128] = eye
             m[one] = jnp.full((2, 8, 512), HIDDEN, F32)
             acc[one] = jnp.zeros((2, 144, 512), F32)
 
@@ -335,7 +339,7 @@
             total = (acc[w_one, w_g].reshape(18, 8, 512) * jnp.exp2((old - new) * SCALE)[None]).reshape(144, 512)
         for j in range(3):
             keys = slice(j * 256, (j + 1) * 256)
-            fresh = dot(b["kx"][block, from_core, keys, :], queries, ((1,), (1,)))
+            fresh = dot(b["kx"][block, from_core, keys, :], queries)
             scores[u][keys, :] = fresh
             top = jnp.maximum(top, jnp.max(fresh.reshape(32, 8, 512), axis=0))
             if weigh:
@@ -560,20 +564,19 @@
             10: both(lambda: g_tkv.have_right(0), lambda: g_tkv.far(0)),
             11: lambda: g_tkv.have_far(0),
             12: lambda: s_context(0),
-            15: lambda: s_context(1),
-            16: lambda: g_tkv.have_own(1),
-            17: both(lambda: g_tkv.mid(1), lambda: g_s.mid(0)),
-            18: lambda: g_tkv.have_left(1),
-            19: both(lambda: g_s.mid(1), lambda: g_s.far(0)),
-            20: lambda: g_tkv.have_right(1),
-            21: both(lambda: g_tkv.far(1), lambda: g_s.far(1)),
-            22: both(lambda: g_tkv.have_far(1), s_sums),
+            16: both(lambda: g_tkv.have_own(1), lambda: s_context(1)),
+            17: lambda: g_tkv.mid(1),
+            18: both(lambda: g_tkv.have_left(1), lambda: g_s.mid(0)),
+            20: both(lambda: g_tkv.have_right(1), lambda: g_s.mid(1), lambda: g_s.far(0)),
+            21: lambda: g_tkv.far(1),
+            22: both(lambda: g_tkv.have_far(1), lambda: g_s.far(1)),
             23: lambda: t_context(0),
         }
     )
     for load in map_loads:
         load.start()
     t_context(1)
+    s_sums()
     r_s.send_on()
     g_t[0].mid(0)
     g_t[0].root(1)

time: 157 us -> 155 us (0.987)
  Pallas kernels: 154 us -> 152 us
    pallas_call x1, Pallas kernels: 154 us -> 152 us  [per_device(): pl.pallas_call(kernel, out_shape=jax.ShapeDtypeStruct((512, 512), F32), i...]
where the time goes in v5:
time: 155 us
  Pallas kernels  152 us (98%)
  local copies, waits for them, and re-layouts  2.26 us (1%)
    pallas_call x1, Pallas kernels, per_device(): pl.pallas_call(kernel, out_shape=jax.ShapeDtypeStruct((512, 512), F32), i...  152 us

profile of v5, /device:TPU:0, one launch (start us, length us, event | category | flops | bytes accessed | tf_op | source)
XLA Modules:
  0.0 154.9 jit_solution(4699258545897803835)
XLA Ops:
  0.7 152.0 %shard_map.118 = f32[512,512]{1,0:T(8,128)} custom-call(s32[1]{0:T(128)S(6)} %copy.14.doc, bf16[128,1024]{1,0:T(8,128)(2,1)} %tq.1, bf16[2,768,128]{2,1,0:T(8,128)(2,1)} %tkv_h.1, bf16[128,512]{1,0:T(8,128)(2,1)} %sq.1, bf16[2,768,128]{2,1,0:T(8,128)(2,1)} %skv_h.1, bf16[256,512]{1,0:T(8,128)(2,1)} %tres.1, bf16[1024,512]{1,0:T(8,128)(2,1)} %tw_h.1, ...), custom_call_target="tpu_custom_call" | custom-call | tf_op jit(solution)/shard_map/pallas_call | solution.py:685
  152.7 2.3 %copy.15 = f32[512,512]{1,0:T(8,128)} copy(f32[512,512]{1,0:T(8,128)} %shard_map.118) | data formatting | bytes 2097152

commit v6 on v5

--- a/solution.py
+++ b/solution.py
@@ -55,7 +55,7 @@
             self.on_right.append(wire.copy(first, first, right))
             self.on_left.append(wire.copy(second, second, left))
             if self.core:
-                refs = [own, block(plane, 3, None), block(plane, 1, None), block(plane, 2, 0), block(plane, 2, 1)]
+                refs = [own, block(plane, 3, None), block(plane, 1, None), block(plane, 2, None)]
                 self.pass_on.append([wire.copy(ref, ref, core) for ref in refs])
 
     def root(self, plane, start_cross=True):
@@ -80,11 +80,9 @@
 
     def far(self, plane):
         self.on_right[plane].wait_recv()
+        self.on_left[plane].wait_recv()
         if self.core:
             self.pass_on[plane][3].start()
-        self.on_left[plane].wait_recv()
-        if self.core:
-            self.pass_on[plane][4].start()
 
     def have_own(self, plane):
         self.pass_on[plane][0].wait_recv()
@@ -101,7 +99,6 @@
 
     def have_far(self, plane):
         self.pass_on[plane][3].wait_recv()
-        self.pass_on[plane][4].wait_recv()
 
 
 def dot(a, b, dims=((1,), (0,)), precision=None):
@@ -121,6 +118,11 @@
         top1=V((8, 512), F32),
         qa=V((3, 2, 256, 512), BF),
         sq_in=V((128, 512), BF),
+        tq_in=V((128, 1024), BF),
+        to_out=V((2, 128, 512), BF),
+        to_in=V((2, 128, 512), BF),
+        tl_out=V((2, 8, 512), F32),
+        tl_in=V((2, 8, 512), F32),
         m=V((3, 2, 8, 512), F32),
         acc=V((3, 2, 144, 512), F32),
         o_out=V((2, 128, 512), BF),
@@ -147,8 +149,10 @@
         sz_in=V((2, 2, 256, 256), BF),
         thid=V((2, 128, 512), F32),
         shid=V((256, 256), F32),
-        tsq=V((2, 16, 8, 128), F32),
-        ssq=V((16, 8, 256), F32),
+        tsq=V((2, 8, 8, 128), F32),
+        ssq=V((8, 8, 256), F32),
+        tsq_chip=V((2, 2, 8, 128), F32),
+        ssq_chip=V((2, 8, 256), F32),
         nb=V((16, 256, 256), BF),
         ng=V((8, 2, 256, 256), BF),
         dl=V((2, 8, 128, 512), BF),
@@ -198,6 +202,7 @@
 
     wire = Wire(b["wsend"], b["wrecv"])
     give_sq = wire.copy(sq, b["sq_in"], across)
+    give_tq = wire.copy(tq, b["tq_in"], core)
 
     def kv_block(model):
         def block(plane, off, part):
@@ -239,26 +244,29 @@
         return block
 
     g_skv = Gather(wire, kv_block(0), right, left, None, core)
-    g_tkv = Gather(wire, kv_block(1), right, left, across, core)
+    g_tkv = Gather(wire, kv_block(1), right, left, across)
     keys_sent = len(wire.made)
     g_s = Gather(wire, s_block, right, left, None, core, 2)
     g_t = [Gather(wire, t_block(half), right, left, across, core) for half in range(2)]
     contexts_sent = len(wire.made)
     g_n = Gather(wire, nb_block, right, left, across, core)
     g_d = [Gather(wire, dl_block(half), tp_dev(0, 1), tp_dev(0, 3), tp_dev(1, 0), None) for half in range(2)]
+    give_to = [wire.copy(b["to_out"].at[i], b["to_in"].at[i], core) for i in range(2)]
+    give_tl = [wire.copy(b["tl_out"].at[i], b["tl_in"].at[i], core) for i in range(2)]
     give_o = [wire.copy(b["o_out"].at[1 - g], b["o_in"].at[g], across) for g in range(2)]
     give_l = [wire.copy(b["l_out"].at[1 - g], b["l_in"].at[g], across) for g in range(2)]
-    s_sq = [wire.copy(b["ssq"].at[s], b["ssq"].at[s], ((s + off) % 16, p)) for off in range(1, 16)]
-    t_sq = [
-        [wire.copy(b["tsq"].at[half, s], b["tsq"].at[half, s], ((s + off) % 16, p)) for off in range(1, 16)]
-        for half in range(2)
-    ]
+    def square_copies(chip, sq):
+        between = wire.copy(chip.at[c], chip.at[c], core)
+        offs = range(1, 8)
+        spread = [wire.copy(sq.at[k_own], sq.at[k_own], (((k_own + off) % 8) * 2 + c, p)) for off in offs]
+        return chip, sq, between, spread
+
+    s_sq = square_copies(b["ssq_chip"], b["ssq"])
+    t_sq = [square_copies(b["tsq_chip"].at[half], b["tsq"].at[half]) for half in range(2)]
     n_tp = [
         wire.copy(b["nb"].at[((p + off) % 8) * 2 + c], b["ng"].at[p, c], (s, (p + off) % 8)) for off in range(1, 8)
     ]
-    n_core = [
-        wire.copy(b["ng"].at[(p + 8 - off) % 8, c], b["ng"].at[(p + 8 - off) % 8, c], core) for off in range(1, 8)
-    ]
+    n_core = wire.copy(b["ng"].at[:, c], b["ng"].at[:, c], core)
 
     qa, m, acc = b["qa"], b["m"], b["acc"]
     heads, tokens = (4, 8, 8), (128, 64, 64)
@@ -278,7 +286,7 @@
         lanes = lax.broadcasted_iota(jnp.int32, (128, 128), 1)
         for one in passes:
             eye = jnp.where(lanes % tokens[one] + 64 * (one // 2) == rows, 1.0, 0.0).astype(BF)
-            for g in range(2 if one == 0 else 1):
+            for g in range(2):
                 for i in range(4):
                     qa[one, g, 128:256, i * 128 : (i + 1) * 128] = eye
             m[one] = jnp.full((2, 8, 512), HIDDEN, F32)
@@ -293,7 +301,7 @@
 
     first_key = doc[0]
 
-    def tile_at(n, u):
+    def tile_at(n):
         third = n // 8
         t = (third + 1) // 2
         other = third // 2
@@ -301,26 +309,27 @@
         i = (1 - t + other) * ((n % 8) // 2) + (t - other) * (n % 4)
         plane = (yh + other) % 2
         at = (x + 3 * i + 3 * (i // 2) + 2 * (i // 3)) % 4
-        from_core = (c + (1 - t) * (n % 2) + t * u) % 2
-        return one, (1 - t) * u, t * (4 + plane * 4) + at, plane, at, from_core
-
-    def build(n, u):
-        one, g, block, plane, at, from_core = tile_at(n, u)
+        return one, t, t * (4 + plane * 4) + at, plane, at, (c + (1 - t) * (n % 2)) % 2
+
+    def build(n, g):
+        one, t, block, plane, at, from_core = tile_at(n)
         base = (plane * 4 + at) * KEYS_CHIP + from_core * 768
 
-        @pl.when((one <= 1) if u == 0 else (one == 1))
+        if g == 0:
+
+            @pl.when(one <= 1)
+            def _():
+                b["vt"][block, from_core, 0:128, :] = b["kv"][block, from_core, 1].T
+                b["kx"][block, from_core, :, 0:128] = b["kv"][block, from_core, 0]
+
+                @pl.when(plane == 0)
+                def _():
+                    key = lax.broadcasted_iota(jnp.int32, (768, 128), 0)
+                    b["kx"][block, from_core, :, 128:256] = jnp.where(key >= first_key - base, 0.0, HIDDEN).astype(BF)
+
+        @pl.when((plane == 1) & (at >= 2))
         def _():
-            b["vt"][block, from_core, 0:128, :] = b["kv"][block, from_core, 1].T
-            b["kx"][block, from_core, :, 0:128] = b["kv"][block, from_core, 0]
-
-            @pl.when(plane == 0)
-            def _():
-                key = lax.broadcasted_iota(jnp.int32, (768, 128), 0)
-                b["kx"][block, from_core, :, 128:256] = jnp.where(key >= first_key - base, 0.0, HIDDEN).astype(BF)
-
-        @pl.when((one <= 1) & (plane == 1) & (at >= 2))
-        def _():
-            ahead = CACHE + ((((yh + g) % 2) * 4 + x) * 2 + c) * 128 - base
+            ahead = CACHE + ((((yh + (1 - t) * g) % 2) * 4 + x) * 2 + (c + t * g) % 2) * 128 - base
             key = lax.broadcasted_iota(jnp.int32, (768, 128), 0)
             row = lax.broadcasted_iota(jnp.int32, (768, 128), 1)
             b["kx"][block, from_core, :, 128:256] = jnp.where(key - row <= ahead, 0.0, HIDDEN).astype(BF)
@@ -328,11 +337,12 @@
     scores, tops = (b["score0"], b["score1"]), (b["top0"], b["top1"])
 
     def overlapped(n, u, weigh_n, weigh=True):
-        one, g, block, _, _, from_core = tile_at(n, u)
-        queries = qa[one, g]
+        one, _, block, _, _, from_core = tile_at(n)
+        queries = qa[one, u]
         top = jnp.full((8, 512), HIDDEN, F32)
         if weigh:
-            w_one, w_g, w_block, _, _, w_core = tile_at(weigh_n, 1 - u)
+            w_one, _, w_block, _, _, w_core = tile_at(weigh_n)
+            w_g = 1 - u
             old = m[w_one, w_g]
             peak = jnp.max(tops[1 - u][...], axis=0, keepdims=True)
             new = jnp.maximum(old, jnp.broadcast_to(peak, (8, 512)))
@@ -387,18 +397,29 @@
             held = both[h * count : (h + 1) * count, :]
             ctx[plane * 4 + x, c, first : first + count, h * 128 : (h + 1) * 128] = held
 
+    def joined(one, g, o_in, l_in):
+        mine, log_mine = part_of(one, g)
+        share = 1.0 / (1.0 + jnp.exp2(log_mine - l_in[...]))
+        other = o_in[...].astype(F32)
+        return mine + ((other - mine).reshape(16, 8, 512) * share[None]).reshape(128, 512)
+
     def s_context(g):
         give_o[g].wait_recv()
         give_l[g].wait_recv()
-        mine, log_mine = part_of(0, g)
-        share = 1.0 / (1.0 + jnp.exp2(log_mine - b["l_in"][g]))
-        other = b["o_in"][g].astype(F32)
-        both = mine + ((other - mine).reshape(16, 8, 512) * share[None]).reshape(128, 512)
-        keep_context(0, (yh + g) % 2, both, b["sctx"])
+        keep_context(0, (yh + g) % 2, joined(0, g, b["o_in"].at[g], b["l_in"].at[g]), b["sctx"])
         g_s.root(g)
 
+    def t_part(half):
+        mean, logs = part_of(1 + half, 1)
+        b["to_out"][half] = mean.astype(BF)
+        b["tl_out"][half] = logs
+        give_to[half].start()
+        give_tl[half].start()
+
     def t_context(half):
-        keep_context(1 + half, yh, part_of(1 + half, 0)[0], b["tctx"])
+        give_to[half].wait_recv()
+        give_tl[half].wait_recv()
+        keep_context(1 + half, yh, joined(1 + half, 0, b["to_in"].at[half], b["tl_in"].at[half]), b["tctx"])
         g_t[half].root(0)
 
     class Reduce:
@@ -472,18 +493,23 @@
             self.beside.wait_recv()
             self.hid[...] = total + self.y_in[...].astype(F32)
 
-    def send_squares(hid, sq, copies):
+    def send_squares(hid, squares):
+        chip, sq, between, spread = squares
         value = hid[...]
         ones = jnp.ones((8, value.shape[1]), F32)
-        sq[s] = dot(ones, value * value, ((1,), (1,)), lax.Precision.HIGHEST)
-        for made in copies:
+        chip[c] = dot(ones, value * value, ((1,), (1,)), lax.Precision.HIGHEST)
+        between.start()
+        between.wait_recv()
+        sq[k_own] = chip[0] + chip[1]
+        for made in spread:
             made.start()
 
-    def inverse_scale(sq, copies, width):
-        for made in copies:
+    def inverse_scale(squares, width):
+        _, sq, _, spread = squares
+        for made in spread:
             made.wait_recv()
         total = sq[0]
-        for i in range(1, 16):
+        for i in range(1, 8):
             total = total + sq[i]
         first = jnp.where(lax.broadcasted_iota(jnp.int32, (8, 128), 0) == 0, 1.0, 0.0)
         column = dot(total, first, ((0,), (0,)), lax.Precision.HIGHEST)
@@ -504,6 +530,7 @@
     pl.semaphore_wait(barrier, 22)
     g_skv.root(0)
     give_sq.start()
+    give_tq.start()
     g_tkv.cross.start()
 
     def s_partner():
@@ -515,12 +542,14 @@
         prepare(4, 12, (1, 2))
         fill_queries(1, tq, 0)
         fill_queries(2, tq, 0)
+        give_tq.wait_recv()
+        fill_queries(1, b["tq_in"], 1)
+        fill_queries(2, b["tq_in"], 1)
         g_skv.mid(0)
         g_tkv.root(0, False)
 
     def t_start():
         partner_part()
-        g_tkv.have_own(0)
         g_tkv.mid(0)
         g_tkv.root(1)
 
@@ -531,10 +560,10 @@
 
     def s_squares():
         r_s.finish(sres)
-        send_squares(b["shid"], b["ssq"], s_sq)
+        send_squares(b["shid"], s_sq)
 
     def s_normed():
-        inverse = inverse_scale(b["ssq"], s_sq, D_S)
+        inverse = inverse_scale(s_sq, D_S)
         inverse = jnp.concatenate([inverse, inverse], axis=1)
         normed = (b["shid"][...] * inverse * sg[...]).astype(BF)
         for at, first in enumerate((0, 128, 64, 192)):
@@ -560,21 +589,21 @@
             5: lambda: g_skv.far(0),
             6: lambda: g_skv.have_far(0),
             8: t_start,
-            9: lambda: g_tkv.have_left(0),
-            10: both(lambda: g_tkv.have_right(0), lambda: g_tkv.far(0)),
-            11: lambda: g_tkv.have_far(0),
+            10: lambda: g_tkv.far(0),
             12: lambda: s_context(0),
-            16: both(lambda: g_tkv.have_own(1), lambda: s_context(1)),
+            16: lambda: s_context(1),
             17: lambda: g_tkv.mid(1),
-            18: both(lambda: g_tkv.have_left(1), lambda: g_s.mid(0)),
-            20: both(lambda: g_tkv.have_right(1), lambda: g_s.mid(1), lambda: g_s.far(0)),
+            18: lambda: g_s.mid(0),
+            20: both(lambda: g_s.mid(1), lambda: g_s.far(0)),
             21: lambda: g_tkv.far(1),
-            22: both(lambda: g_tkv.have_far(1), lambda: g_s.far(1)),
-            23: lambda: t_context(0),
+            22: lambda: g_s.far(1),
+            23: lambda: t_part(0),
         }
     )
     for load in map_loads:
         load.start()
+    t_part(1)
+    t_context(0)
     t_context(1)
     s_sums()
     r_s.send_on()
@@ -600,7 +629,7 @@
     g_n.mid(0)
     g_n.root(1)
     r_t[0].finish(tres)
-    send_squares(b["thid"].at[0], b["tsq"].at[0], t_sq[0])
+    send_squares(b["thid"].at[0], t_sq[0])
     g_n.far(0)
     g_n.mid(1)
     r_t[1].settle()
@@ -608,7 +637,7 @@
     for made in n_tp:
         made.start()
     r_t[1].finish(tres)
-    send_squares(b["thid"].at[1], b["tsq"].at[1], t_sq[1])
+    send_squares(b["thid"].at[1], t_sq[1])
     wire.close(keys_sent, contexts_sent)
     ready(g_n, 0)
     ready(g_n, 1)
@@ -625,7 +654,7 @@
     lax.fori_loop(0, 8, match, 0)
 
     def delta(half):
-        inverse = inverse_scale(b["tsq"].at[half], t_sq[half], D_T)
+        inverse = inverse_scale(t_sq[half], D_T)
         inverse = jnp.concatenate([inverse, inverse, inverse, inverse], axis=1)
         target = b["thid"][half] * inverse * tg[...]
         b["dl"][half, p] = ((b["diff"][half] - target) * (1.0 / math.sqrt(SLAB))).astype(BF)
@@ -645,18 +674,16 @@
     own, near, far = (0, 1, 1), (1, 2, 2), (2, 1, 1)
     delta(0)
     delta(1)
-    b["ng"][p, 0] = b["nb"][2 * p]
-    b["ng"][p, 1] = b["nb"][2 * p + 1]
+    b["ng"][p, c] = b["nb"][2 * p + c]
     out[...] = jnp.zeros((512, 512), F32)
     g_d[0].mid(0)
     g_d[0].root(1)
-    for made, onward in zip(n_tp, n_core):
+    for made in n_tp:
         made.wait_recv()
-        onward.start()
+    n_core.start()
     g_d[0].far(0)
     g_d[0].mid(1)
-    for made in n_core:
-        made.wait_recv()
+    n_core.wait_recv()
     gradient(0, 0, own)
     gradient(0, 0, near)
     gradient(0, 0, far)

time: 155 us -> 154 us (level)
  Pallas kernels: 152 us -> 150 us
    pallas_call x1, Pallas kernels: 152 us -> 150 us  [per_device(): pl.pallas_call(kernel, out_shape=jax.ShapeDtypeStruct((512, 512), F32), i...]
where the time goes in v6:
time: 154 us; the launch traced here: 153 us
  Pallas kernels  150 us (97%)
  local copies, waits for them, and re-layouts  2.26 us (1%)
    pallas_call x1, Pallas kernels, per_device(): pl.pallas_call(kernel, out_shape=jax.ShapeDtypeStruct((512, 512), F32), i...  150 us

profile of v6, /device:TPU:0, one launch (start us, length us, event | category | flops | bytes accessed | tf_op | source)
XLA Modules:
  0.0 153.1 jit_solution(4919910503228234184)
XLA Ops:
  0.7 150.2 %shard_map.118 = f32[512,512]{1,0:T(8,128)} custom-call(s32[1]{0:T(128)S(6)} %copy.14.doc, bf16[128,1024]{1,0:T(8,128)(2,1)} %tq.1, bf16[2,768,128]{2,1,0:T(8,128)(2,1)} %tkv_h.1, bf16[128,512]{1,0:T(8,128)(2,1)} %sq.1, bf16[2,768,128]{2,1,0:T(8,128)(2,1)} %skv_h.1, bf16[256,512]{1,0:T(8,128)(2,1)} %tres.1, bf16[1024,512]{1,0:T(8,128)(2,1)} %tw_h.1, ...), custom_call_target="tpu_custom_call" | custom-call | tf_op jit(solution)/shard_map/pallas_call | solution.py:712
  150.8 2.3 %copy.15 = f32[512,512]{1,0:T(8,128)} copy(f32[512,512]{1,0:T(8,128)} %shard_map.118) | data formatting | bytes 2097152

commit v7 on v6

--- a/solution.py
+++ b/solution.py
@@ -632,26 +632,19 @@
     send_squares(b["thid"].at[0], t_sq[0])
     g_n.far(0)
     g_n.mid(1)
-    r_t[1].settle()
-    g_n.far(1)
-    for made in n_tp:
-        made.start()
-    r_t[1].finish(tres)
-    send_squares(b["thid"].at[1], t_sq[1])
-    wire.close(keys_sent, contexts_sent)
-    ready(g_n, 0)
-    ready(g_n, 1)
     b["diff"][...] = jnp.zeros((2, 128, 512), F32)
     for load in map_loads:
         load.wait()
 
-    def match(k, carry):
-        lhs = jnp.concatenate([b["nb"][2 * k], b["nb"][2 * k + 1]], axis=1)
-        for u in range(2):
-            b["diff"][:, :, u * 256 : (u + 1) * 256] += dot(lhs, b["kx"][k, u, 0:512, :]).reshape(2, 128, 256)
-        return carry
-
-    lax.fori_loop(0, 8, match, 0)
+    def match(plane):
+        def one(i, carry):
+            k = ((yh + plane) % 2) * 4 + i
+            lhs = jnp.concatenate([b["nb"][2 * k], b["nb"][2 * k + 1]], axis=1)
+            for u in range(2):
+                b["diff"][:, :, u * 256 : (u + 1) * 256] += dot(lhs, b["kx"][k, u, 0:512, :]).reshape(2, 128, 256)
+            return carry
+
+        lax.fori_loop(0, 4, one, 0)
 
     def delta(half):
         inverse = inverse_scale(t_sq[half], D_T)
@@ -660,48 +653,50 @@
         b["dl"][half, p] = ((b["diff"][half] - target) * (1.0 / math.sqrt(SLAB))).astype(BF)
         g_d[half].root(0)
 
-    def gradient(half, plane, offs):
+    def gradient(plane, offs):
         def one(i, carry):
             q = ((z + offs[0] + i * offs[1]) % 4) * 2 + (yl + plane) % 2
+            deltas = b["dl"][:, q].reshape(256, 512)
             for at in range(2):
-                rows = slice(at * 256, (at + 1) * 256)
-                lhs = b["ng"][q, at, half * 128 : (half + 1) * 128, :]
-                out[rows, :] += dot(lhs, b["dl"][half, q], ((0,), (0,)))
+                out[at * 256 : (at + 1) * 256, :] += dot(b["ng"][q, at], deltas, ((0,), (0,)))
             return carry
 
         lax.fori_loop(0, offs[2], one, 0)
 
     own, near, far = (0, 1, 1), (1, 2, 2), (2, 1, 1)
+    ready(g_n, 0)
+    match(0)
+    r_t[1].settle()
+    g_n.far(1)
+    for made in n_tp:
+        made.start()
+    ready(g_n, 1)
+    match(1)
     delta(0)
-    delta(1)
+    r_t[1].finish(tres)
+    send_squares(b["thid"].at[1], t_sq[1])
     b["ng"][p, c] = b["nb"][2 * p + c]
     out[...] = jnp.zeros((512, 512), F32)
-    g_d[0].mid(0)
-    g_d[0].root(1)
+    delta(1)
+    for half in range(2):
+        g_d[half].mid(0)
+        g_d[half].root(1)
     for made in n_tp:
         made.wait_recv()
     n_core.start()
-    g_d[0].far(0)
-    g_d[0].mid(1)
+    for half in range(2):
+        g_d[half].far(0)
+        g_d[half].mid(1)
+    wire.close(keys_sent, contexts_sent)
     n_core.wait_recv()
-    gradient(0, 0, own)
-    gradient(0, 0, near)
-    gradient(0, 0, far)
-    gradient(0, 1, own)
-    g_d[1].mid(0)
-    g_d[1].root(1)
-    gradient(0, 1, near)
-    g_d[0].far(1)
-    gradient(0, 1, far)
-    gradient(1, 0, own)
-    gradient(1, 0, near)
-    gradient(1, 1, own)
-    g_d[1].far(0)
-    g_d[1].mid(1)
-    gradient(1, 0, far)
-    gradient(1, 1, near)
-    g_d[1].far(1)
-    gradient(1, 1, far)
+    gradient(0, own)
+    gradient(0, near)
+    gradient(0, far)
+    gradient(1, own)
+    gradient(1, near)
+    for half in range(2):
+        g_d[half].far(1)
+    gradient(1, far)
     wire.close()
 
 

time: 154 us -> 155 us (level)
  Pallas kernels: 150 us -> 152 us
where the time goes in v7:
time: 155 us
  Pallas kernels  152 us (98%)
  local copies, waits for them, and re-layouts  2.26 us (1%)
    pallas_call x1, Pallas kernels, per_device(): pl.pallas_call(kernel, out_shape=jax.ShapeDtypeStruct((512, 512), F32), i...  152 us

profile of v7, /device:TPU:0, one launch (start us, length us, event | category | flops | bytes accessed | tf_op | source)
XLA Modules:
  0.0 154.6 jit_solution(5257052348238685702)
XLA Ops:
  0.7 151.6 %shard_map.118 = f32[512,512]{1,0:T(8,128)} custom-call(s32[1]{0:T(128)S(6)} %copy.14.doc, bf16[128,1024]{1,0:T(8,128)(2,1)} %tq.1, bf16[2,768,128]{2,1,0:T(8,128)(2,1)} %tkv_h.1, bf16[128,512]{1,0:T(8,128)(2,1)} %sq.1, bf16[2,768,128]{2,1,0:T(8,128)(2,1)} %skv_h.1, bf16[256,512]{1,0:T(8,128)(2,1)} %tres.1, bf16[1024,512]{1,0:T(8,128)(2,1)} %tw_h.1, ...), custom_call_target="tpu_custom_call" | custom-call | tf_op jit(solution)/shard_map/pallas_call | solution.py:707
  152.3 2.3 %copy.15 = f32[512,512]{1,0:T(8,128)} copy(f32[512,512]{1,0:T(8,128)} %shard_map.118) | data formatting | bytes 2097152

commit v8 on v7

--- a/solution.py
+++ b/solution.py
@@ -157,6 +157,8 @@
         ng=V((8, 2, 256, 256), BF),
         dl=V((2, 8, 128, 512), BF),
         diff=V((2, 128, 512), F32),
+        nts=D((8,)),
+        ntr=D((8,)),
         wsend=D((200,)),
         wrecv=D((200,)),
         loc=D((8,)),
@@ -263,9 +265,29 @@
 
     s_sq = square_copies(b["ssq_chip"], b["ssq"])
     t_sq = [square_copies(b["tsq_chip"].at[half], b["tsq"].at[half]) for half in range(2)]
-    n_tp = [
-        wire.copy(b["nb"].at[((p + off) % 8) * 2 + c], b["ng"].at[p, c], (s, (p + off) % 8)) for off in range(1, 8)
-    ]
+    def give_normed(q):
+        return pltpu.make_async_remote_copy(
+            src_ref=b["nb"].at[q * 2 + c], dst_ref=b["ng"].at[p, c], send_sem=b["nts"].at[q], recv_sem=b["ntr"].at[p],
+            device_id=(s, q), device_id_type=MESH,
+        )
+
+    def start_normed(plane):
+        for i in range(4):
+            q = ((yh + plane) % 2) * 4 + i
+            pl.when(q != p)(lambda q=q: give_normed(q).start())
+
+    def have_normed():
+        for off in range(1, 8):
+            q = (p + off) % 8
+            pltpu.make_async_remote_copy(
+                src_ref=b["ng"].at[q, c], dst_ref=b["ng"].at[q, c], send_sem=b["nts"].at[q],
+                recv_sem=b["ntr"].at[q], device_id=(s, q), device_id_type=MESH,
+            ).wait_recv()
+
+    def close_normed():
+        for off in range(1, 8):
+            give_normed((p + off) % 8).wait_send()
+
     n_core = wire.copy(b["ng"].at[:, c], b["ng"].at[:, c], core)
 
     qa, m, acc = b["qa"], b["m"], b["acc"]
@@ -632,6 +654,7 @@
     send_squares(b["thid"].at[0], t_sq[0])
     g_n.far(0)
     g_n.mid(1)
+    start_normed(0)
     b["diff"][...] = jnp.zeros((2, 128, 512), F32)
     for load in map_loads:
         load.wait()
@@ -668,8 +691,7 @@
     match(0)
     r_t[1].settle()
     g_n.far(1)
-    for made in n_tp:
-        made.start()
+    start_normed(1)
     ready(g_n, 1)
     match(1)
     delta(0)
@@ -681,8 +703,7 @@
     for half in range(2):
         g_d[half].mid(0)
         g_d[half].root(1)
-    for made in n_tp:
-        made.wait_recv()
+    have_normed()
     n_core.start()
     for half in range(2):
         g_d[half].far(0)
@@ -697,6 +718,7 @@
     for half in range(2):
         g_d[half].far(1)
     gradient(1, far)
+    close_normed()
     wire.close()
 
 

time: 155 us -> 155 us (level)
  no operation moved by 1% of the time
where the time goes in v8:
time: 155 us; the launch traced here: 154 us
  Pallas kernels  151 us (97%)
  local copies, waits for them, and re-layouts  2.26 us (1%)
    pallas_call x1, Pallas kernels, per_device(): pl.pallas_call(kernel, out_shape=jax.ShapeDtypeStruct((512, 512), F32), i...  151 us

profile of v8, /device:TPU:0, one launch (start us, length us, event | category | flops | bytes accessed | tf_op | source)
XLA Modules:
  0.0 154.0 jit_solution(12549540381396545801)
XLA Ops:
  0.7 151.1 %shard_map.118 = f32[512,512]{1,0:T(8,128)} custom-call(s32[1]{0:T(128)S(6)} %copy.14.doc, bf16[128,1024]{1,0:T(8,128)(2,1)} %tq.1, bf16[2,768,128]{2,1,0:T(8,128)(2,1)} %tkv_h.1, bf16[128,512]{1,0:T(8,128)(2,1)} %sq.1, bf16[2,768,128]{2,1,0:T(8,128)(2,1)} %skv_h.1, bf16[256,512]{1,0:T(8,128)(2,1)} %tres.1, bf16[1024,512]{1,0:T(8,128)(2,1)} %tw_h.1, ...), custom_call_target="tpu_custom_call" | custom-call | tf_op jit(solution)/shard_map/pallas_call | solution.py:729
  151.7 2.3 %copy.15 = f32[512,512]{1,0:T(8,128)} copy(f32[512,512]{1,0:T(8,128)} %shard_map.118) | data formatting | bytes 2097152

commit v9 on v6

--- a/solution.py
+++ b/solution.py
@@ -347,14 +347,14 @@
             peak = jnp.max(tops[1 - u][...], axis=0, keepdims=True)
             new = jnp.maximum(old, jnp.broadcast_to(peak, (8, 512)))
             total = (acc[w_one, w_g].reshape(18, 8, 512) * jnp.exp2((old - new) * SCALE)[None]).reshape(144, 512)
-        for j in range(3):
-            keys = slice(j * 256, (j + 1) * 256)
+        for first, count in ((0, 512), (512, 256)):
+            keys = slice(first, first + count)
             fresh = dot(b["kx"][block, from_core, keys, :], queries)
             scores[u][keys, :] = fresh
-            top = jnp.maximum(top, jnp.max(fresh.reshape(32, 8, 512), axis=0))
+            top = jnp.maximum(top, jnp.max(fresh.reshape(count // 8, 8, 512), axis=0))
             if weigh:
-                held = scores[1 - u][keys, :].reshape(32, 8, 512)
-                weights = jnp.exp2((held - new[None]) * SCALE).reshape(256, 512).astype(BF)
+                held = scores[1 - u][keys, :].reshape(count // 8, 8, 512)
+                weights = jnp.exp2((held - new[None]) * SCALE).reshape(count, 512).astype(BF)
                 total = total + dot(b["vt"][w_block, w_core, :, keys], weights)
         tops[u][...] = top
         if weigh:

time: 154 us -> 154 us (level)
  no operation moved by 1% of the time
where the time goes in v9:
time: 154 us; the launch traced here: 153 us
  Pallas kernels  150 us (97%)
  local copies, waits for them, and re-layouts  2.26 us (1%)
    pallas_call x1, Pallas kernels, per_device(): pl.pallas_call(kernel, out_shape=jax.ShapeDtypeStruct((512, 512), F32), i...  150 us

profile of v9, /device:TPU:0, one launch (start us, length us, event | category | flops | bytes accessed | tf_op | source)
XLA Modules:
  0.0 153.2 jit_solution(14707935180947612571)
XLA Ops:
  0.7 150.3 %shard_map.118 = f32[512,512]{1,0:T(8,128)} custom-call(s32[1]{0:T(128)S(6)} %copy.14.doc, bf16[128,1024]{1,0:T(8,128)(2,1)} %tq.1, bf16[2,768,128]{2,1,0:T(8,128)(2,1)} %tkv_h.1, bf16[128,512]{1,0:T(8,128)(2,1)} %sq.1, bf16[2,768,128]{2,1,0:T(8,128)(2,1)} %skv_h.1, bf16[256,512]{1,0:T(8,128)(2,1)} %tres.1, bf16[1024,512]{1,0:T(8,128)(2,1)} %tw_h.1, ...), custom_call_target="tpu_custom_call" | custom-call | tf_op jit(solution)/shard_map/pallas_call | solution.py:712
  151.0 2.3 %copy.15 = f32[512,512]{1,0:T(8,128)} copy(f32[512,512]{1,0:T(8,128)} %shard_map.118) | data formatting | bytes 2097152

commit v10 on v6

--- a/solution.py
+++ b/solution.py
@@ -549,9 +549,9 @@
         g_tkv.root(0, False)
 
     def t_start():
-        partner_part()
         g_tkv.mid(0)
         g_tkv.root(1)
+        partner_part()
 
     def s_sums():
         for load in loads[2:]:
@@ -591,8 +591,8 @@
             8: t_start,
             10: lambda: g_tkv.far(0),
             12: lambda: s_context(0),
-            16: lambda: s_context(1),
-            17: lambda: g_tkv.mid(1),
+            16: lambda: g_tkv.mid(1),
+            17: lambda: s_context(1),
             18: lambda: g_s.mid(0),
             20: both(lambda: g_s.mid(1), lambda: g_s.far(0)),
             21: lambda: g_tkv.far(1),

time: 154 us -> 154 us (level)
  no operation moved by 1% of the time
where the time goes in v10:
time: 154 us; the launch traced here: 153 us
  Pallas kernels  150 us (97%)
  local copies, waits for them, and re-layouts  2.26 us (1%)
    pallas_call x1, Pallas kernels, per_device(): pl.pallas_call(kernel, out_shape=jax.ShapeDtypeStruct((512, 512), F32), i...  150 us

profile of v10, /device:TPU:0, one launch (start us, length us, event | category | flops | bytes accessed | tf_op | source)
XLA Modules:
  0.0 153.0 jit_solution(17479976591677835612)
XLA Ops:
  0.7 150.1 %shard_map.118 = f32[512,512]{1,0:T(8,128)} custom-call(s32[1]{0:T(128)S(6)} %copy.14.doc, bf16[128,1024]{1,0:T(8,128)(2,1)} %tq.1, bf16[2,768,128]{2,1,0:T(8,128)(2,1)} %tkv_h.1, bf16[128,512]{1,0:T(8,128)(2,1)} %sq.1, bf16[2,768,128]{2,1,0:T(8,128)(2,1)} %skv_h.1, bf16[256,512]{1,0:T(8,128)(2,1)} %tres.1, bf16[1024,512]{1,0:T(8,128)(2,1)} %tw_h.1, ...), custom_call_target="tpu_custom_call" | custom-call | tf_op jit(solution)/shard_map/pallas_call | solution.py:712
  150.8 2.3 %copy.15 = f32[512,512]{1,0:T(8,128)} copy(f32[512,512]{1,0:T(8,128)} %shard_map.118) | data formatting | bytes 2097152
